TPU v7x, 32 devices: a whole 2x2x4 slice. The times are simulated.
32 devices in a mesh: sec: 4 (over y, core), tile: 8 (over z, x).
Axes of the slice: x: 2, y: 2, z: 4, core: 2. Of those that a mesh axis runs over, the one named last changes fastest.
Arguments:
- tile_strips: bfloat16 [4, 8, 2, 5, 64, 512], P('sec', 'tile'), may hold values from -6 to 6, as said below
- pair_mask: int32 [4, 8, 2, 3], P('sec', 'tile'), may hold values 0 or 1
- strip_offset: int32 [4, 8, 2, 3, 2], P('sec', 'tile'), may hold values from -16 to 16
- stiffness: float32 [4, 8, 2], P('sec', 'tile'), may hold values from 0.05 to 0.5
Outputs:
- affine_update: float32 [6, 4, 8, 2], P(None, 'sec', 'tile')
- residual: float32 [6, 4, 8, 2], P(None, 'sec', 'tile')
Inputs may be any that keep to these rules, and one draw needn't show every extreme that they name: `tile_strips`: neighbouring tiles' intersecting images are correlated.
All inputs are finite; a program needn't handle non-finite values. No bound on the sum of `pair_mask` on one device may be relied on, other than what follows from the above.
Results may differ from a plain program's by a relative error of at most 0.0013.
Values may be sent and summed in bfloat16 or wider, within the bound.
A program may use at most 64 MiB of HBM per device.

v0:
```python
import jax
import jax.numpy as jnp
from jax import lax
from jax.sharding import PartitionSpec as P

ITERS = 3


highest = lax.Precision.HIGHEST


def passed_along(shard, axis, by):
    length = lax.axis_size(axis)
    pairs = [(i, i + by) for i in range(length) if 0 <= i + by < length]
    return lax.ppermute(shard, axis, pairs)


def with_halo(cells, sides, width):
    for axis, dim in sides:
        count = lax.axis_size(axis)
        ends = count - 1
        head = lax.slice_in_dim(cells, 0, width, axis=dim)
        tail = lax.slice_in_dim(cells, cells.shape[dim] - width, cells.shape[dim], axis=dim)
        cells = jnp.concatenate(
            [
                lax.ppermute(tail, axis, [(i, (i + 1) % count) for i in range(ends)]),
                cells,
                lax.ppermute(head, axis, [((i + 1) % count, i) for i in range(ends)]),
            ],
            axis=dim,
        )
    return cells


def strip_gradients(image):
    padded = jnp.pad(image, 1)
    along_x = (padded[1:-1, 2:] - padded[1:-1, :-2]) * 0.5
    along_y = (padded[2:, 1:-1] - padded[:-2, 1:-1]) * 0.5
    return (along_x, along_y)


def jacobian_rows(image, shift_x, shift_y):
    height, width = image.shape
    column_grid = jnp.arange(width, dtype=jnp.float32)[None, :]
    row_grid = jnp.arange(height, dtype=jnp.float32)[:, None]
    coord_u = (column_grid + shift_x) / width - 0.5
    coord_v = (row_grid + shift_y) / height - 0.5
    along_x, along_y = strip_gradients(image)
    stacked = jnp.stack(
        [
            along_x * coord_u,
            along_x * coord_v,
            along_x,
            along_y * coord_u,
            along_y * coord_v,
            along_y,
        ]
    )
    return stacked.reshape(6, height * width)


def pair_block(image_a, image_b, offset):
    first = image_a.astype(jnp.float32)
    second = image_b.astype(jnp.float32)
    shifts = offset.astype(jnp.float32)
    zero = jnp.zeros((), jnp.float32)
    jacobian = jnp.concatenate(
        [jacobian_rows(first, zero, zero), -jacobian_rows(second, shifts[0], shifts[1])], axis=0
    )
    pixels = first.shape[0] * first.shape[1]
    misfit = (first - second).reshape(pixels)
    normal = (
        jnp.dot(jacobian, jacobian.T, precision=highest, preferred_element_type=jnp.float32)
        / pixels
    )
    pull = (
        -jnp.dot(jacobian, misfit, precision=highest, preferred_element_type=jnp.float32) / pixels
    )
    return (normal, pull)


def to_next(array, axis):
    lead = jnp.zeros_like(lax.slice_in_dim(array, 0, 1, axis=axis))
    return jnp.concatenate(
        [lead, lax.slice_in_dim(array, 0, array.shape[axis] - 1, axis=axis)], axis=axis
    )


def from_next(array, axis):
    tail = jnp.zeros_like(lax.slice_in_dim(array, 0, 1, axis=axis))
    return jnp.concatenate(
        [lax.slice_in_dim(array, 1, array.shape[axis], axis=axis), tail], axis=axis
    )


def apply_block(block, vector):
    return jnp.einsum("ij...,j...->i...", block, vector, precision=highest)


def cholesky_rows(matrix):
    order = matrix.shape[0]
    factor = [[None] * order for index in range(order)]
    for column in range(order):
        pivot = matrix[column, column]
        for inner in range(column):
            pivot = pivot - factor[column][inner] * factor[column][inner]
        pivot = jnp.sqrt(pivot)
        factor[column][column] = pivot
        for row in range(column + 1, order):
            entry = matrix[row, column]
            for inner in range(column):
                entry = entry - factor[row][inner] * factor[column][inner]
            factor[row][column] = entry / pivot
    return factor


def solve_rows(factor, vector):
    order = len(factor)
    forward = []
    for row in range(order):
        value = vector[row]
        for inner in range(row):
            value = value - factor[row][inner] * forward[inner]
        forward.append(value / factor[row][row])
    backward = [None] * order
    for row in reversed(range(order)):
        value = forward[row]
        for inner in range(row + 1, order):
            value = value - factor[inner][row] * backward[inner]
        backward[row] = value / factor[row][row]
    return jnp.stack(backward)


def tile_blocks(images_a, images_b, offsets, exists):
    normal, pull = lax.map(
        lambda items: pair_block(items[0], items[1], items[2]), (images_a, images_b, offsets)
    )
    return (jnp.transpose(normal, (1, 2, 0)) * exists, jnp.transpose(pull, (1, 0)) * exists)


def paired_sum(residual, scaled, product):
    return lax.psum((jnp.sum(residual * scaled), jnp.sum(scaled * product)), ("sec", "tile"))


def shards(tile_strips, pair_mask, strip_offset, stiffness):
    columns = tile_strips.shape[2]
    sections = lax.axis_size("sec")
    tile_rows = lax.axis_size("tile")
    section = lax.axis_index("sec")
    tile_row = lax.axis_index("tile")
    strips = tile_strips[0, 0]
    masks = pair_mask[0, 0]
    offsets = strip_offset[0, 0]
    column_index = jnp.arange(columns)
    exists_right = ((masks[:, 0] == 1) & (column_index < columns - 1)).astype(jnp.float32)
    exists_down = ((masks[:, 1] == 1) & (tile_row < tile_rows - 1)).astype(jnp.float32)
    exists_cross = ((masks[:, 2] == 1) & (section < sections - 1)).astype(jnp.float32)
    normal_right, pull_right = tile_blocks(
        strips[:, 1], from_next(strips[:, 0], 0), offsets[:, 0], exists_right
    )
    lower_top = passed_along(strips[:, 2], "tile", -1)
    normal_down, pull_down = tile_blocks(strips[:, 3], lower_top, offsets[:, 1], exists_down)
    later_patch = passed_along(strips[:, 4], "sec", -1)
    normal_cross, pull_cross = tile_blocks(strips[:, 4], later_patch, offsets[:, 2], exists_cross)
    upper_down = passed_along((normal_down[6:, 6:], normal_down[:6, 6:], pull_down[6:]), "tile", 1)
    upper_cross = passed_along(
        (normal_cross[6:, 6:], normal_cross[:6, 6:], pull_cross[6:]), "sec", 1
    )
    identity = jnp.eye(6, dtype=jnp.float32)[:, :, None]
    diagonal = (
        stiffness[0, 0][None, None, :] * identity
        + normal_right[:6, :6]
        + to_next(normal_right[6:, 6:], 2)
    )
    diagonal = diagonal + normal_down[:6, :6] + upper_down[0]
    diagonal = diagonal + normal_cross[:6, :6] + upper_cross[0]
    load = pull_right[:6] + to_next(pull_right[6:], 1) + pull_down[:6] + upper_down[2]
    load = load + pull_cross[:6] + upper_cross[2]
    coupling_right = normal_right[:6, 6:]
    coupling_down = normal_down[:6, 6:]
    coupling_cross = normal_cross[:6, 6:]

    def multiply(vector):
        spread = with_halo(vector[:, None, None, :], (("sec", 1), ("tile", 2)), 1)
        result = apply_block(diagonal, vector)
        result = result + apply_block(coupling_right, from_next(vector, 1))
        result = result + to_next(apply_block(jnp.swapaxes(coupling_right, 0, 1), vector), 1)
        result = result + apply_block(coupling_down, spread[:, 1, 2])
        result = result + apply_block(jnp.swapaxes(upper_down[1], 0, 1), spread[:, 1, 0])
        result = result + apply_block(coupling_cross, spread[:, 2, 1])
        result = result + apply_block(jnp.swapaxes(upper_cross[1], 0, 1), spread[:, 0, 1])
        return result

    factor = cholesky_rows(diagonal)
    affine_update = jnp.zeros_like(load)
    residual = load
    scaled = solve_rows(factor, residual)
    product = multiply(scaled)
    rho_now, curve = paired_sum(residual, scaled, product)
    step_size = rho_now / curve
    direction, carried = (scaled, product)
    for step in range(ITERS):
        affine_update = affine_update + step_size * direction
        residual = residual - step_size * carried
        if step + 1 < ITERS:
            scaled = solve_rows(factor, residual)
            product = multiply(scaled)
            rho_next, curve = paired_sum(residual, scaled, product)
            factor_next = rho_next / rho_now
            step_size = rho_next / (curve - factor_next * rho_next / step_size)
            direction = scaled + factor_next * direction
            carried = product + factor_next * carried
            rho_now = rho_next
    return (affine_update.reshape(6, 1, 1, columns), residual.reshape(6, 1, 1, columns))


def solution(mesh):
    return jax.shard_map(
        shards,
        mesh=mesh,
        in_specs=(
            P("sec", "tile", None, None, None, None),
            P("sec", "tile", None, None),
            P("sec", "tile", None, None, None),
            P("sec", "tile", None),
        ),
        out_specs=(P(None, "sec", "tile", None), P(None, "sec", "tile", None)),
        check_vma=False,
    )
```

profile of v0, /device:TPU:0, one launch (start us, length us, event | category | flops | bytes accessed | tf_op | source)
XLA Modules:
  0.0 361.0 jit_solution(1374407759809343391)
XLA Ops:
  7.9 41.4 %while.45 = (s32[]{:T(128)}, f32[2,12,12]{2,1,0:T(8,128)S(1)}, f32[2,12]{1,0:T(2,128)}, bf16[2,64,512]{2,1,0:T(8,128)(2,1)}, bf16[2,64,512]{2,1,0:T(8,128)(2,1)}, /*index=5*/s32[2,2]{1,0:T(2,128)}, s32[]{:T(128)}, s32[]{:T(128)}) while((s32[]{:T(128)}, f32[2,12,12]{2,1,0:T(8,128)S(1)}, f32[2,12]{1,0:T(2,128)}, bf16[2,64,512]{2,1,0:T(8,128)(2,1)}, ...), condition=%wide.region_1.2_spmd, body=%wide.region_0.1_spmd.sunk | while | flops 62232948 | bytes 19164288 | solution.py:135
  18.6 3.9 %concatenate.128 = f32[12,32768]{1,0:T(8,128)S(1)} concatenate(f32[1,32768]{1,0:T(1,128)S(1)} %bitcast.711, f32[1,32768]{1,0:T(1,128)S(1)} %bitcast.714, f32[1,32768]{1,0:T(1,128)} %bitcast.717, f32[1,32768]{1,0:T(1,128)} %bitcast.720, f32[1,32768]{1,0:T(1,128)} %bitcast.723, f32[1,32768]{1,0:T(1,128)} %bitcast.726, f32[6,32768]{1,0:T(8,128)S(1)} %neg.64), dimensions={0} | concatenate | bytes 3145728 | tf_op jit(solution)/shard_map/while/body/eval_jaxpr/concatenate | solution.py:67
  39.4 3.9 %concatenate.128 = f32[12,32768]{1,0:T(8,128)S(1)} concatenate(f32[1,32768]{1,0:T(1,128)S(1)} %bitcast.711, f32[1,32768]{1,0:T(1,128)S(1)} %bitcast.714, f32[1,32768]{1,0:T(1,128)} %bitcast.717, f32[1,32768]{1,0:T(1,128)} %bitcast.720, f32[1,32768]{1,0:T(1,128)} %bitcast.723, f32[1,32768]{1,0:T(1,128)} %bitcast.726, f32[6,32768]{1,0:T(8,128)S(1)} %neg.64), dimensions={0} | concatenate | bytes 3145728 | tf_op jit(solution)/shard_map/while/body/eval_jaxpr/concatenate | solution.py:67
  55.3 42.4 %while.46 = (s32[]{:T(128)}, f32[2,12,12]{2,1,0:T(8,128)}, f32[2,12]{1,0:T(2,128)}, bf16[2,64,512]{2,1,0:T(8,128)(2,1)}, bf16[2,64,512]{2,1,0:T(8,128)(2,1)}, /*index=5*/s32[2,2]{1,0:T(2,128)}, s32[]{:T(128)}, s32[]{:T(128)}) while((s32[]{:T(128)}, f32[2,12,12]{2,1,0:T(8,128)}, f32[2,12]{1,0:T(2,128)}, bf16[2,64,512]{2,1,0:T(8,128)(2,1)}, ...), condition=%wide.region_3.4_spmd, body=%wide.region_2.3_spmd.sunk | while | flops 62232948 | bytes 19173560 | solution.py:135
  66.1 3.9 %concatenate.129 = f32[12,32768]{1,0:T(8,128)S(1)} concatenate(f32[1,32768]{1,0:T(1,128)S(1)} %bitcast.712, f32[1,32768]{1,0:T(1,128)S(1)} %bitcast.715, f32[1,32768]{1,0:T(1,128)} %bitcast.718, f32[1,32768]{1,0:T(1,128)} %bitcast.721, f32[1,32768]{1,0:T(1,128)} %bitcast.724, f32[1,32768]{1,0:T(1,128)} %bitcast.727, f32[6,32768]{1,0:T(8,128)S(1)} %neg.66), dimensions={0} | concatenate | bytes 3145728 | tf_op jit(solution)/shard_map/while/body/eval_jaxpr/concatenate | solution.py:67
  87.3 3.9 %concatenate.129 = f32[12,32768]{1,0:T(8,128)S(1)} concatenate(f32[1,32768]{1,0:T(1,128)S(1)} %bitcast.712, f32[1,32768]{1,0:T(1,128)S(1)} %bitcast.715, f32[1,32768]{1,0:T(1,128)} %bitcast.718, f32[1,32768]{1,0:T(1,128)} %bitcast.721, f32[1,32768]{1,0:T(1,128)} %bitcast.724, f32[1,32768]{1,0:T(1,128)} %bitcast.727, f32[6,32768]{1,0:T(8,128)S(1)} %neg.66), dimensions={0} | concatenate | bytes 3145728 | tf_op jit(solution)/shard_map/while/body/eval_jaxpr/concatenate | solution.py:67
  99.9 6.3 %collective-permute-start.1 = (f32[6,2]{0,1:T(2,128)}, f32[6,2]{0,1:T(2,128)}, u32[]{:S(2)}, u32[]{:S(2)}) collective-permute-start(f32[6,2]{0,1:T(2,128)} %slice.471), channel_id=1, source_target_pairs={{0,1},{1,2},{2,3},{3,4},{4,5},{5,6},{6,7},{8,9},{9,10},{10,11},{11... | collective-permute-start | bytes 152 | tf_op jit(solution)/shard_map/ppermute | solution.py:15
  106.9 4.8 %collective-permute-start.10 = (f32[6,6,2]{1,0,2:T(8,128)}, f32[6,6,2]{1,0,2:T(8,128)}, u32[]{:S(2)}, u32[]{:S(2)}) collective-permute-start(f32[6,6,2]{1,0,2:T(8,128)} %get-tuple-element.502), channel_id=1, source_target_pairs={{0,1},{1,2},{2,3},{3,4},{4,5},{5,6},{6,7},{8,9},{9,10},{10,11},{11... | collective-permute-start | bytes 872 | tf_op jit(solution)/shard_map/ppermute | solution.py:15
  115.5 42.8 %while.47 = (s32[]{:T(128)}, f32[2,12,12]{2,1,0:T(8,128)}, f32[2,12]{1,0:T(2,128)}, bf16[2,64,512]{2,1,0:T(8,128)(2,1)}, bf16[2,64,512]{2,1,0:T(8,128)(2,1)}, /*index=5*/s32[2,2]{1,0:T(2,128)}, s32[]{:T(128)}, s32[]{:T(128)}) while((s32[]{:T(128)}, f32[2,12,12]{2,1,0:T(8,128)}, f32[2,12]{1,0:T(2,128)}, bf16[2,64,512]{2,1,0:T(8,128)(2,1)}, ...), condition=%wide.region_5.6_spmd, body=%wide.region_4.5_spmd.sunk | while | flops 62232948 | bytes 19173560 | solution.py:135
  126.3 3.9 %concatenate.130 = f32[12,32768]{1,0:T(8,128)S(1)} concatenate(f32[1,32768]{1,0:T(1,128)S(1)} %bitcast.713, f32[1,32768]{1,0:T(1,128)S(1)} %bitcast.716, f32[1,32768]{1,0:T(1,128)} %bitcast.719, f32[1,32768]{1,0:T(1,128)} %bitcast.722, f32[1,32768]{1,0:T(1,128)} %bitcast.725, f32[1,32768]{1,0:T(1,128)} %bitcast.728, f32[6,32768]{1,0:T(8,128)S(1)} %neg.68), dimensions={0} | concatenate | bytes 3145728 | tf_op jit(solution)/shard_map/while/body/eval_jaxpr/concatenate | solution.py:67
  147.7 3.9 %concatenate.130 = f32[12,32768]{1,0:T(8,128)S(1)} concatenate(f32[1,32768]{1,0:T(1,128)S(1)} %bitcast.713, f32[1,32768]{1,0:T(1,128)S(1)} %bitcast.716, f32[1,32768]{1,0:T(1,128)} %bitcast.719, f32[1,32768]{1,0:T(1,128)} %bitcast.722, f32[1,32768]{1,0:T(1,128)} %bitcast.725, f32[1,32768]{1,0:T(1,128)} %bitcast.728, f32[6,32768]{1,0:T(8,128)S(1)} %neg.68), dimensions={0} | concatenate | bytes 3145728 | tf_op jit(solution)/shard_map/while/body/eval_jaxpr/concatenate | solution.py:67
  161.9 4.1 %collective-permute-start.11 = (f32[6,6,2]{1,0,2:T(8,128)S(1)}, f32[6,6,2]{1,0,2:T(8,128)S(1)}, u32[]{:S(2)}, u32[]{:S(2)}) collective-permute-start(f32[6,6,2]{1,0,2:T(8,128)S(1)} %get-tuple-element.504), channel_id=1, source_target_pairs={{0,8},{8,16},{16,24},{1,9},{9,17},{17,25},{2,10},{10,18},{18,26},{... | collective-permute-start | bytes 872 | tf_op jit(solution)/shard_map/ppermute | solution.py:15
  171.7 3.0 collective-permute-start.6
  175.6 3.8 %collective-permute-start.9 = (f32[6,3,1,2]{0,3,2,1:T(2,128)S(1)}, f32[6,3,1,2]{0,3,2,1:T(2,128)S(1)}, u32[]{:S(2)}, u32[]{:S(2)}) collective-permute-start(f32[6,3,1,2]{0,3,2,1:T(2,128)S(1)} %pad_maximum_fusion), channel_id=1, source_target_pairs={{0,1},{1,2},{2,3},{3,4},{4,5},{5,6},{6,7},{8,9},{9,10},{10,11},{11... | collective-permute-start | bytes 440 | tf_op jit(solution)/shard_map/ppermute | solution.py:26
  181.0 3.8 %collective-permute-done.8 = f32[6,3,1,2]{0,3,2,1:T(2,128)S(1)} collective-permute-done((f32[6,3,1,2]{0,3,2,1:T(2,128)S(1)}, f32[6,3,1,2]{0,3,2,1:T(2,128)S(1)}, u32[]{:S(2)}, u32[]{:S(2)}) %collective-permute-start.8) | collective-permute-done | bytes 176 | tf_op jit(solution)/shard_map/ppermute | solution.py:28
  187.3 43.5 %all-reduce.17 = (f32[]{:T(128)}, f32[]{:T(128)}) all-reduce(f32[]{:T(128)} %get-tuple-element.323, f32[]{:T(128)} %get-tuple-element.322), channel_id=1, replica_groups=mesh['sec'=4,'tile'=8] {'sec','tile'}, use_global_device_ids=true, to_apply=%region_7.8 | all-reduce | flops 2 | bytes 16 | tf_op jit(solution)/shard_map/psum | solution.py:142
  234.1 3.0 collective-permute-start.12
  237.9 4.2 %collective-permute-start.15 = (f32[6,3,1,2]{0,3,2,1:T(2,128)S(1)}, f32[6,3,1,2]{0,3,2,1:T(2,128)S(1)}, u32[]{:S(2)}, u32[]{:S(2)}) collective-permute-start(f32[6,3,1,2]{0,3,2,1:T(2,128)S(1)} %pad_maximum_fusion.1), channel_id=1, source_target_pairs={{0,1},{1,2},{2,3},{3,4},{4,5},{5,6},{6,7},{8,9},{9,10},{10,11},{11... | collective-permute-start | bytes 440 | tf_op jit(solution)/shard_map/ppermute | solution.py:26
  243.7 3.8 %collective-permute-done.14 = f32[6,3,1,2]{0,3,2,1:T(2,128)S(1)} collective-permute-done((f32[6,3,1,2]{0,3,2,1:T(2,128)S(1)}, f32[6,3,1,2]{0,3,2,1:T(2,128)S(1)}, u32[]{:S(2)}, u32[]{:S(2)}) %collective-permute-start.14) | collective-permute-done | bytes 176 | tf_op jit(solution)/shard_map/ppermute | solution.py:28
  250.0 41.4 %all-reduce.16 = (f32[]{:T(128)}, f32[]{:T(128)}) all-reduce(f32[]{:T(128)} %get-tuple-element.321, f32[]{:T(128)} %get-tuple-element.320), channel_id=1, replica_groups=mesh['sec'=4,'tile'=8] {'sec','tile'}, use_global_device_ids=true, to_apply=%region_11.12 | all-reduce | flops 2 | bytes 16 | tf_op jit(solution)/shard_map/psum | solution.py:142
  297.8 3.0 collective-permute-start.16
  301.7 4.2 %collective-permute-start.19 = (f32[6,3,1,2]{0,3,2,1:T(2,128)S(1)}, f32[6,3,1,2]{0,3,2,1:T(2,128)S(1)}, u32[]{:S(2)}, u32[]{:S(2)}) collective-permute-start(f32[6,3,1,2]{0,3,2,1:T(2,128)S(1)} %pad_maximum_fusion.2), channel_id=1, source_target_pairs={{0,1},{1,2},{2,3},{3,4},{4,5},{5,6},{6,7},{8,9},{9,10},{10,11},{11... | collective-permute-start | bytes 440 | tf_op jit(solution)/shard_map/ppermute | solution.py:26
  307.5 3.8 %collective-permute-done.18 = f32[6,3,1,2]{0,3,2,1:T(2,128)S(1)} collective-permute-done((f32[6,3,1,2]{0,3,2,1:T(2,128)S(1)}, f32[6,3,1,2]{0,3,2,1:T(2,128)S(1)}, u32[]{:S(2)}, u32[]{:S(2)}) %collective-permute-start.18) | collective-permute-done | bytes 176 | tf_op jit(solution)/shard_map/ppermute | solution.py:28
  313.7 42.3 %all-reduce.15 = (f32[]{:T(128)}, f32[]{:T(128)}) all-reduce(f32[]{:T(128)} %get-tuple-element.319, f32[]{:T(128)} %get-tuple-element.318), channel_id=1, replica_groups=mesh['sec'=4,'tile'=8] {'sec','tile'}, use_global_device_ids=true, to_apply=%region_15.16 | all-reduce | flops 2 | bytes 16 | tf_op jit(solution)/shard_map/psum | solution.py:142
  (350 shorter events, 151.1 us)
Async XLA Ops:
  0.6 5.2 %copy-start.6 = (s32[1,1,2,3,2]{3,4,2,1,0:T(2,128)S(1)}, s32[1,1,2,3,2]{3,4,2,1,0:T(2,128)}, u32[]{:S(2)}) copy-start(s32[1,1,2,3,2]{3,4,2,1,0:T(2,128)} %param.12) | copy-start | bytes 148
  2.6 51.5 %collective-permute-start = (bf16[2,64,512]{2,1,0:T(8,128)(2,1)}, bf16[2,64,512]{2,1,0:T(8,128)(2,1)}, u32[]{:S(2)}, u32[]{:S(2)}) collective-permute-start(bf16[2,64,512]{2,1,0:T(8,128)(2,1)} %get-tuple-element.500), channel_id=1, source_target_pairs={{1,0},{2,1},{3,2},{4,3},{5,4},{6,5},{7,6},{9,8},{10,9},{11,10},{12... | collective-permute-start | bytes 393224 | tf_op jit(solution)/shard_map/ppermute | solution.py:15
  3.9 110.4 %collective-permute-start.2 = (bf16[2,64,512]{2,1,0:T(8,128)(2,1)}, bf16[2,64,512]{2,1,0:T(8,128)(2,1)}, u32[]{:S(2)}, u32[]{:S(2)}) collective-permute-start(bf16[2,64,512]{2,1,0:T(8,128)(2,1)} %get-tuple-element.738), channel_id=1, source_target_pairs={{8,0},{16,8},{24,16},{9,1},{17,9},{25,17},{10,2},{18,10},{26,18},{... | collective-permute-start | bytes 393224 | tf_op jit(solution)/shard_map/ppermute | solution.py:15
  50.0 5.3 %copy-start.9 = (f32[12,2]{0,1:T(2,128)}, f32[12,2]{0,1:T(2,128)S(1)}, u32[]{:S(2)}) copy-start(f32[12,2]{0,1:T(2,128)S(1)} %multiply_bitcast_fusion.41) | copy-start | bytes 292
  98.5 8.4 %copy-start.7 = (f32[12,2]{0,1:T(2,128)}, f32[12,2]{0,1:T(2,128)S(1)}, u32[]{:S(2)}) copy-start(f32[12,2]{0,1:T(2,128)S(1)} %multiply_bitcast_fusion.40) | copy-start | bytes 292
  99.3 6.9 %copy-start = (f32[12,12,2]{1,0,2:T(8,128)}, f32[12,12,2]{1,0,2:T(8,128)S(1)}, u32[]{:S(2)}) copy-start(f32[12,12,2]{1,0,2:T(8,128)S(1)} %multiply_bitcast_fusion.37) | copy-start | bytes 3460
  99.9 66.1 %collective-permute-start.1 = (f32[6,2]{0,1:T(2,128)}, f32[6,2]{0,1:T(2,128)}, u32[]{:S(2)}, u32[]{:S(2)}) collective-permute-start(f32[6,2]{0,1:T(2,128)} %slice.471), channel_id=1, source_target_pairs={{0,1},{1,2},{2,3},{3,4},{4,5},{5,6},{6,7},{8,9},{9,10},{10,11},{11... | collective-permute-start | bytes 152 | tf_op jit(solution)/shard_map/ppermute | solution.py:15
  106.9 78.9 %collective-permute-start.10 = (f32[6,6,2]{1,0,2:T(8,128)}, f32[6,6,2]{1,0,2:T(8,128)}, u32[]{:S(2)}, u32[]{:S(2)}) collective-permute-start(f32[6,6,2]{1,0,2:T(8,128)} %get-tuple-element.502), channel_id=1, source_target_pairs={{0,1},{1,2},{2,3},{3,4},{4,5},{5,6},{6,7},{8,9},{9,10},{10,11},{11... | collective-permute-start | bytes 872 | tf_op jit(solution)/shard_map/ppermute | solution.py:15
  111.7 57.0 %collective-permute-start.4 = (f32[6,6,2]{1,0,2:T(8,128)}, f32[6,6,2]{1,0,2:T(8,128)}, u32[]{:S(2)}, u32[]{:S(2)}) collective-permute-start(f32[6,6,2]{1,0,2:T(8,128)} %get-tuple-element.503), channel_id=1, source_target_pairs={{0,1},{1,2},{2,3},{3,4},{4,5},{5,6},{6,7},{8,9},{9,10},{10,11},{11... | collective-permute-start | bytes 872 | tf_op jit(solution)/shard_map/ppermute | solution.py:15
  159.9 8.0 %collective-permute-start.3 = (f32[6,2]{0,1:T(2,128)S(1)}, f32[6,2]{0,1:T(2,128)S(1)}, u32[]{:S(2)}, u32[]{:S(2)}) collective-permute-start(f32[6,2]{0,1:T(2,128)S(1)} %slice.476), channel_id=1, source_target_pairs={{0,8},{8,16},{16,24},{1,9},{9,17},{17,25},{2,10},{10,18},{18,26},{... | collective-permute-start | bytes 152 | tf_op jit(solution)/shard_map/ppermute | solution.py:15
  161.9 19.0 %collective-permute-start.11 = (f32[6,6,2]{1,0,2:T(8,128)S(1)}, f32[6,6,2]{1,0,2:T(8,128)S(1)}, u32[]{:S(2)}, u32[]{:S(2)}) collective-permute-start(f32[6,6,2]{1,0,2:T(8,128)S(1)} %get-tuple-element.504), channel_id=1, source_target_pairs={{0,8},{8,16},{16,24},{1,9},{9,17},{17,25},{2,10},{10,18},{18,26},{... | collective-permute-start | bytes 872 | tf_op jit(solution)/shard_map/ppermute | solution.py:15
  166.0 2.7 collective-permute-start.5
  170.4 4.7 %collective-permute-start.7 = (f32[6,1,1,2]{0,3,2,1:T(2,128)S(1)}, f32[6,1,1,2]{0,3,2,1:T(2,128)S(1)}, u32[]{:S(2)}, u32[]{:S(2)}) collective-permute-start(f32[6,1,1,2]{0,3,2,1:T(2,128)S(1)} %bitcast.740), channel_id=1, source_target_pairs={{8,0},{16,8},{24,16},{9,1},{17,9},{25,17},{10,2},{18,10},{26,18},{... | collective-permute-start | bytes 152 | tf_op jit(solution)/shard_map/ppermute | solution.py:28
  171.7 3.8 %collective-permute-start.6 = (f32[6,1,1,2]{0,3,2,1:T(2,128)S(1)}, f32[6,1,1,2]{0,3,2,1:T(2,128)S(1)}, u32[]{:S(2)}, u32[]{:S(2)}) collective-permute-start(f32[6,1,1,2]{0,3,2,1:T(2,128)S(1)} %bitcast.741), channel_id=1, source_target_pairs={{0,8},{8,16},{16,24},{1,9},{9,17},{17,25},{2,10},{10,18},{18,26},{... | collective-permute-start | bytes 152 | tf_op jit(solution)/shard_map/ppermute | solution.py:26
  175.6 10.2 %collective-permute-start.9 = (f32[6,3,1,2]{0,3,2,1:T(2,128)S(1)}, f32[6,3,1,2]{0,3,2,1:T(2,128)S(1)}, u32[]{:S(2)}, u32[]{:S(2)}) collective-permute-start(f32[6,3,1,2]{0,3,2,1:T(2,128)S(1)} %pad_maximum_fusion), channel_id=1, source_target_pairs={{0,1},{1,2},{2,3},{3,4},{4,5},{5,6},{6,7},{8,9},{9,10},{10,11},{11... | collective-permute-start | bytes 440 | tf_op jit(solution)/shard_map/ppermute | solution.py:26
  179.4 5.5 %collective-permute-start.8 = (f32[6,3,1,2]{0,3,2,1:T(2,128)S(1)}, f32[6,3,1,2]{0,3,2,1:T(2,128)S(1)}, u32[]{:S(2)}, u32[]{:S(2)}) collective-permute-start(f32[6,3,1,2]{0,3,2,1:T(2,128)S(1)} %pad_maximum_fusion), channel_id=1, source_target_pairs={{1,0},{2,1},{3,2},{4,3},{5,4},{6,5},{7,6},{9,8},{10,9},{11,10},{12... | collective-permute-start | bytes 440 | tf_op jit(solution)/shard_map/ppermute | solution.py:28
  232.8 4.7 %collective-permute-start.13 = (f32[6,1,1,2]{0,3,2,1:T(2,128)S(1)}, f32[6,1,1,2]{0,3,2,1:T(2,128)S(1)}, u32[]{:S(2)}, u32[]{:S(2)}) collective-permute-start(f32[6,1,1,2]{0,3,2,1:T(2,128)S(1)} %bitcast.750), channel_id=1, source_target_pairs={{8,0},{16,8},{24,16},{9,1},{17,9},{25,17},{10,2},{18,10},{26,18},{... | collective-permute-start | bytes 152 | tf_op jit(solution)/shard_map/ppermute | solution.py:28
  234.1 3.8 %collective-permute-start.12 = (f32[6,1,1,2]{0,3,2,1:T(2,128)S(1)}, f32[6,1,1,2]{0,3,2,1:T(2,128)S(1)}, u32[]{:S(2)}, u32[]{:S(2)}) collective-permute-start(f32[6,1,1,2]{0,3,2,1:T(2,128)S(1)} %bitcast.751), channel_id=1, source_target_pairs={{0,8},{8,16},{16,24},{1,9},{9,17},{17,25},{2,10},{10,18},{18,26},{... | collective-permute-start | bytes 152 | tf_op jit(solution)/shard_map/ppermute | solution.py:26
  237.9 10.6 %collective-permute-start.15 = (f32[6,3,1,2]{0,3,2,1:T(2,128)S(1)}, f32[6,3,1,2]{0,3,2,1:T(2,128)S(1)}, u32[]{:S(2)}, u32[]{:S(2)}) collective-permute-start(f32[6,3,1,2]{0,3,2,1:T(2,128)S(1)} %pad_maximum_fusion.1), channel_id=1, source_target_pairs={{0,1},{1,2},{2,3},{3,4},{4,5},{5,6},{6,7},{8,9},{9,10},{10,11},{11... | collective-permute-start | bytes 440 | tf_op jit(solution)/shard_map/ppermute | solution.py:26
  242.1 5.5 %collective-permute-start.14 = (f32[6,3,1,2]{0,3,2,1:T(2,128)S(1)}, f32[6,3,1,2]{0,3,2,1:T(2,128)S(1)}, u32[]{:S(2)}, u32[]{:S(2)}) collective-permute-start(f32[6,3,1,2]{0,3,2,1:T(2,128)S(1)} %pad_maximum_fusion.1), channel_id=1, source_target_pairs={{1,0},{2,1},{3,2},{4,3},{5,4},{6,5},{7,6},{9,8},{10,9},{11,10},{12... | collective-permute-start | bytes 440 | tf_op jit(solution)/shard_map/ppermute | solution.py:28
  296.5 4.7 %collective-permute-start.17 = (f32[6,1,1,2]{0,3,2,1:T(2,128)S(1)}, f32[6,1,1,2]{0,3,2,1:T(2,128)S(1)}, u32[]{:S(2)}, u32[]{:S(2)}) collective-permute-start(f32[6,1,1,2]{0,3,2,1:T(2,128)S(1)} %bitcast.745), channel_id=1, source_target_pairs={{8,0},{16,8},{24,16},{9,1},{17,9},{25,17},{10,2},{18,10},{26,18},{... | collective-permute-start | bytes 152 | tf_op jit(solution)/shard_map/ppermute | solution.py:28
  297.8 3.8 %collective-permute-start.16 = (f32[6,1,1,2]{0,3,2,1:T(2,128)S(1)}, f32[6,1,1,2]{0,3,2,1:T(2,128)S(1)}, u32[]{:S(2)}, u32[]{:S(2)}) collective-permute-start(f32[6,1,1,2]{0,3,2,1:T(2,128)S(1)} %bitcast.746), channel_id=1, source_target_pairs={{0,8},{8,16},{16,24},{1,9},{9,17},{17,25},{2,10},{10,18},{18,26},{... | collective-permute-start | bytes 152 | tf_op jit(solution)/shard_map/ppermute | solution.py:26
  301.7 10.6 %collective-permute-start.19 = (f32[6,3,1,2]{0,3,2,1:T(2,128)S(1)}, f32[6,3,1,2]{0,3,2,1:T(2,128)S(1)}, u32[]{:S(2)}, u32[]{:S(2)}) collective-permute-start(f32[6,3,1,2]{0,3,2,1:T(2,128)S(1)} %pad_maximum_fusion.2), channel_id=1, source_target_pairs={{0,1},{1,2},{2,3},{3,4},{4,5},{5,6},{6,7},{8,9},{9,10},{10,11},{11... | collective-permute-start | bytes 440 | tf_op jit(solution)/shard_map/ppermute | solution.py:26
  305.9 5.5 %collective-permute-start.18 = (f32[6,3,1,2]{0,3,2,1:T(2,128)S(1)}, f32[6,3,1,2]{0,3,2,1:T(2,128)S(1)}, u32[]{:S(2)}, u32[]{:S(2)}) collective-permute-start(f32[6,3,1,2]{0,3,2,1:T(2,128)S(1)} %pad_maximum_fusion.2), channel_id=1, source_target_pairs={{1,0},{2,1},{3,2},{4,3},{5,4},{6,5},{7,6},{9,8},{10,9},{11,10},{12... | collective-permute-start | bytes 440 | tf_op jit(solution)/shard_map/ppermute | solution.py:28
  (22 other events, 38.7 us)
where the time goes:
time: 364 us; the launch traced here: 361 us
  blocking collectives  127 us (35%)
  local copies, waits for them, and re-layouts  81.7 us (22%)
  starting transfers between devices  53.2 us (15%)
  matrix products  40.5 us (11%)
  other arithmetic  33.7 us (9%)
  waiting for transfers between devices  13.1 us (4%)
  between operations  10.5 us (3%)
    psum x3, blocking collectives, paired_sum(): lax.psum((jnp.sum(residual * scaled), jnp.sum(scaled * product)), ('sec',...  127 us
    while x118, local copies, waits for them, and re-layouts  32 us
    ppermute x8, starting transfers between devices, passed_along(): return lax.ppermute(shard, axis, pairs)  24.2 us
    concatenate x6, local copies, waits for them, and re-layouts, pair_block(): jnp.concatenate([jacobian_rows(first, zero, zero), -jacobian_rows(second,...  23.2 us
    ppermute x6, starting transfers between devices, with_halo(): lax.ppermute(tail, axis, [(i, (i + 1) % count) for i in range(ends)])  21.2 us
    dot_general x6, matrix products, pair_block(): jnp.dot(jacobian, jacobian.T, precision=highest, preferred_element_type=j...  17.1 us
    dot_general x6, matrix products, pair_block(): jnp.dot(jacobian, misfit, precision=highest, preferred_element_type=jnp.f...  15.5 us
    ppermute x6, waiting for transfers between devices, with_halo(): lax.ppermute(head, axis, [((i + 1) % count, i) for i in range(ends)])  11.5 us
  transfers between devices with their start and end apart: 20, of which 7 were waited for; matrix products, arithmetic and copies ran while one was open for 39% of the time, Pallas kernels for 0%

commit v1 on v0

v1 whole, which is shorter than its diff:
```python
import functools

import jax
import jax.numpy as jnp
from jax import lax
from jax.experimental import pallas as pl
from jax.experimental.pallas import tpu as pltpu
from jax.sharding import PartitionSpec as P

ITERS = 3
LANES = 128
SUB = 8
IMAGES = 5
KINDS = 3
BLOCK = 6 * SUB
QROWS = 4
MESH = pl.DeviceIdType.MESH

PLACES = (
    ((2, 2),),
    ((0, 2), (2, 0)),
    ((1, 2), (2, 1)),
    ((0, 0),),
    ((0, 1), (1, 0)),
    ((1, 1),),
)
SELF_AT = tuple((image // 2, BLOCK * (image % 2)) for image in range(IMAGES))
PAIR_AT = ((2, BLOCK), (3, 0), (3, BLOCK))
PULL_AT = ((2, 96), (3, 96), (3, 112))
OFFSET_AT = (0, 96)
STIFF_AT = (0, 120)
EXISTS_AT = (1, 96)
ENDS = ((1, 0), (3, 2), (4, 4))


def round_up(value, unit):
    return (value + unit - 1) // unit * unit


def column_moments(fields, width, quadratic):
    groups = fields.groups
    sums = None
    for k in range(groups):
        values = fields(k)
        if sums is None:
            sums = [[value] * (3 if quadratic else 2) for value in values]
        else:
            for entry, value in zip(sums, values):
                entry[0] = entry[0] + value
                entry[1] = entry[1] + entry[0]
                if quadratic:
                    entry[2] = entry[2] + entry[1]
    height = groups * SUB
    step = SUB / height
    row = lax.broadcasted_iota(jnp.int32, (SUB, width), 0).astype(jnp.float32)
    column = lax.broadcasted_iota(jnp.int32, (SUB, width), 1).astype(jnp.float32)
    edge = row / height + 0.5
    u = column / width - 0.5

    def fold(array):
        total = array[:, :LANES]
        for start in range(LANES, width, LANES):
            total = total + array[:, start : start + LANES]
        return jnp.sum(total, axis=0, keepdims=True)

    out = []
    for entry in sums:
        zeroth = entry[0]
        first = edge * zeroth - step * entry[1]
        scaled = u * zeroth
        moments = [fold(zeroth), fold(scaled), fold(first)]
        if quadratic:
            second = (
                edge * edge * zeroth
                - (2.0 * step) * edge * entry[1]
                + (step * step) * (2.0 * entry[2] - entry[1])
            )
            moments += [fold(u * scaled), fold(u * first), fold(second)]
        out.append(moments)
    return out


class Products:
    def __init__(self, groups, form):
        self.groups = groups
        self.form = form

    def __call__(self, k):
        return self.form(k)


def apply_columns(columns, vector):
    total = columns[0] * vector[0:1]
    for j in range(1, 6):
        total = total + columns[j] * vector[j : j + 1]
    return total


def inverse_columns(columns, sublane):
    columns = list(columns)
    for p in range(6):
        pivot = 1.0 / columns[p][p : p + 1]
        here = sublane == p
        lead = columns[p]
        for j in range(6):
            if j != p:
                ratio = columns[j][p : p + 1] * pivot
                columns[j] = jnp.where(here, ratio, columns[j] - lead * ratio)
        columns[p] = jnp.where(here, pivot, -lead * pivot)
    return columns


def transposed_columns(columns, sublane):
    out = []
    for i in range(6):
        total = jnp.zeros_like(columns[0])
        for j in range(6):
            total = jnp.where(sublane == j, columns[j][i : i + 1], total)
        out.append(total)
    return out


def kernel(
    sections,
    tile_rows,
    strips_hbm,
    mask_ref,
    offset_ref,
    stiff_ref,
    update_ref,
    residual_ref,
    strips,
    landed,
    grad_x,
    grad_y,
    rows,
    gathered,
    local_sem,
    strip_send,
    strip_recv,
    gather_send,
    gather_recv,
):
    columns, _, height, width = strips.shape
    count = sections * tile_rows
    per_device = gathered.shape[0] // count
    groups = height // SUB
    own_images = columns * IMAGES
    section = lax.axis_index("sec")
    tile_row = lax.axis_index("tile")
    me = section * tile_rows + tile_row

    def device(step):
        other = lax.rem(me + step, count)
        return (other // tile_rows, lax.rem(other, tile_rows))

    barrier = pltpu.get_barrier_semaphore()

    @pl.loop(1, count)
    def _(step):
        pl.semaphore_signal(barrier, inc=1, device_id=device(step), device_id_type=MESH)

    local = pltpu.make_async_copy(strips_hbm, strips, local_sem)
    local.start()

    def band(size, sign):
        first = lax.broadcasted_iota(jnp.int32, (size, size), 0)
        second = lax.broadcasted_iota(jnp.int32, (size, size), 1)
        gap = (first - second) * sign
        return jnp.where(gap == 1, 0.5, jnp.where(gap == -1, -0.5, 0.0)).astype(jnp.bfloat16)

    along = band(width, 1)
    down = band(height, -1)
    rows[...] = jnp.zeros_like(rows)

    pl.semaphore_wait(barrier, count - 1)

    def strip_copy(kind, c):
        target = (section, tile_row - 1) if kind == 0 else (section - 1, tile_row)
        return pltpu.make_async_remote_copy(
            src_ref=strips_hbm.at[c, 2 if kind == 0 else 4],
            dst_ref=landed.at[kind, c],
            send_sem=strip_send.at[kind, c],
            recv_sem=strip_recv.at[kind, c],
            device_id=target,
            device_id_type=MESH,
        )

    sends = (tile_row > 0, section > 0)
    receives = (tile_row < tile_rows - 1, section < sections - 1)
    for kind in range(2):

        @pl.when(sends[kind])
        def _():
            for c in range(columns):
                strip_copy(kind, c).start()

    local.wait()

    def gradients(images, start):
        total = images.shape[0] * height
        grad_x[pl.ds(start * height, total), :] = jnp.dot(
            images.reshape(total, width), along, preferred_element_type=jnp.float32
        )
        for index in range(images.shape[0]):
            grad_y[pl.ds((start + index) * height, height), :] = jnp.dot(
                down, images[index], preferred_element_type=jnp.float32
            )

    gradients(strips[...].reshape(own_images, height, width), 0)

    def group(ref, image, k):
        return ref[pl.ds(pl.multiple_of(image * height + k * SUB, SUB), SUB), :]

    def put(row, value):
        rows[pl.ds(row, 1), :] = value

    def self_blocks(c, image, spot):
        at = c * IMAGES + image

        def form(k):
            x, y = group(grad_x, at, k), group(grad_y, at, k)
            return (x * x, x * y, y * y)

        moments = column_moments(Products(groups, form), width, True)
        base = (c * QROWS + spot[0]) * LANES + spot[1]
        for p, q, entry in ((0, 0, moments[0]), (0, 1, moments[1]), (1, 1, moments[2])):
            for places, value in zip(PLACES, entry):
                for a, b in places:
                    put(base + SUB * (3 * q + b) + 3 * p + a, value)
                    if p != q:
                        put(base + SUB * (3 * p + b) + 3 * q + a, value)

    def pair_blocks(kind, c, at_a, at_b, image_a, image_b):
        def cross(k):
            xa, ya = group(grad_x, at_a, k), group(grad_y, at_a, k)
            xb, yb = group(grad_x, at_b, k), group(grad_y, at_b, k)
            return (xa * xb, xa * yb, ya * xb, ya * yb)

        misfit = image_a.astype(jnp.float32) - image_b.astype(jnp.float32)

        def pulls(k):
            miss = misfit[k * SUB : (k + 1) * SUB]
            return (
                group(grad_x, at_a, k) * miss,
                group(grad_y, at_a, k) * miss,
                group(grad_x, at_b, k) * miss,
                group(grad_y, at_b, k) * miss,
            )

        base = (c * QROWS + PAIR_AT[kind][0]) * LANES + PAIR_AT[kind][1]
        for index, entry in enumerate(column_moments(Products(groups, cross), width, True)):
            p, q = divmod(index, 2)
            for places, value in zip(PLACES, entry):
                for a, b in places:
                    put(base + SUB * (3 * q + b) + 3 * p + a, -value)
        base = (c * QROWS + PULL_AT[kind][0]) * LANES + PULL_AT[kind][1]
        for index, entry in enumerate(column_moments(Products(groups, pulls), width, False)):
            side, p = divmod(index, 2)
            for weight, value in zip((2, 0, 1), entry):
                put(base + SUB * side + 3 * p + weight, value if side else -value)

    for image in range(IMAGES):

        @pl.loop(0, columns)
        def _(c):
            self_blocks(c, image, SELF_AT[image])

    @pl.loop(0, columns - 1)
    def _(c):
        pair_blocks(
            0, c, c * IMAGES + 1, (c + 1) * IMAGES, strips[c, 1], strips[c + 1, 0]
        )

    for kind in range(2):

        @pl.when(receives[kind])
        def _():
            for c in range(columns):
                strip_copy(kind, c).wait_recv()
            gradients(landed[kind], own_images + kind * columns)

            @pl.loop(0, columns)
            def _(c):
                image = ENDS[kind + 1][0]
                pair_blocks(
                    kind + 1,
                    c,
                    c * IMAGES + image,
                    own_images + kind * columns + c,
                    strips[c, image],
                    landed[kind, c],
                )

    ones = jnp.ones((SUB, LANES), jnp.bfloat16)
    lane = lax.broadcasted_iota(jnp.int32, (1, LANES), 1)
    contract = (((1,), (1,)), ((), ()))
    mine = pl.multiple_of(me * per_device, SUB)

    def exists(c, kind):
        inside = (jnp.int32(c) < columns - 1, receives[0], receives[1])[kind]
        return jnp.where((mask_ref[c, kind] == 1) & inside, 1.0, 0.0)

    for c in range(columns):
        for h in range(QROWS):
            part = rows[(c * QROWS + h) * LANES : (c * QROWS + h + 1) * LANES, :]
            high = part.astype(jnp.bfloat16)
            low = (part - high.astype(jnp.float32)).astype(jnp.bfloat16)
            summed = lax.dot_general(ones, high, contract, preferred_element_type=jnp.float32)
            summed = summed + lax.dot_general(ones, low, contract, preferred_element_type=jnp.float32)
            line = summed[0:1] * (1.0 / (height * width))
            if h == 0:
                for kind in range(KINDS):
                    start = OFFSET_AT[1] + SUB * kind
                    for axis, extent in ((0, width), (1, height)):
                        shift = offset_ref[c, kind, axis].astype(jnp.float32) / extent
                        here = (lane == start + axis) | (lane == start + 3 + axis)
                        line = jnp.where(here, shift, line)
                line = jnp.where(lane >= STIFF_AT[1], stiff_ref[c], line)
            if h == 1:
                for kind in range(KINDS):
                    start = EXISTS_AT[1] + SUB * kind
                    here = (lane >= start) & (lane < start + SUB)
                    line = jnp.where(here, exists(c, kind), line)
            gathered[pl.ds(mine + c * QROWS + h, 1), :] = line

    @pl.loop(1, count)
    def _(step):
        pltpu.make_async_remote_copy(
            src_ref=gathered.at[pl.ds(mine, per_device)],
            dst_ref=gathered.at[pl.ds(mine, per_device)],
            send_sem=gather_send,
            recv_sem=gather_recv,
            device_id=device(step),
            device_id_type=MESH,
        ).start()

    others = gathered.at[pl.ds(0, (count - 1) * per_device)]
    pltpu.make_async_copy(others, others, gather_recv).wait()

    tiles = columns * count
    padded = round_up(tiles, LANES)
    tables = []
    for h in range(QROWS):
        parts = [
            gathered[pl.ds(c * QROWS + h, count, stride=per_device), :] for c in range(columns)
        ]
        if padded > tiles:
            parts.append(jnp.zeros((padded - tiles, LANES), jnp.float32))
        tables.append(jnp.concatenate(parts, axis=0).T)

    def vector_at(spot, index=0):
        start = spot[1] + SUB * index
        return tables[spot[0]][start : start + SUB]

    def columns_at(spot):
        return [vector_at(spot, j) for j in range(6)]

    sublane = lax.broadcasted_iota(jnp.int32, (SUB, padded), 0)
    place = lax.broadcasted_iota(jnp.int32, (SUB, padded), 1)

    def to_next(array, by):
        return pltpu.roll(array, by, 1)

    def from_next(array, by):
        return pltpu.roll(array, padded - by, 1)

    shifts = (count, 1, tile_rows)
    stiffness = jnp.where(place < tiles, vector_at(STIFF_AT), 1.0)
    diagonal = [jnp.where(sublane == j, stiffness, 0.0) for j in range(6)]
    load = jnp.zeros((SUB, padded), jnp.float32)
    couplings = []
    for kind in range(KINDS):
        by = shifts[kind]
        there = vector_at(EXISTS_AT, kind)
        offset = vector_at(OFFSET_AT, kind)
        du, dv = offset[0:1], offset[1:2]

        def shift_rows(vector):
            return vector + offset * jnp.where(sublane < 3, vector[2:3], vector[5:6])

        def shift_columns(block):
            out = []
            for p in range(2):
                last = block[3 * p + 2]
                out += [block[3 * p] + du * last, block[3 * p + 1] + dv * last, last]
            return out

        block_a = columns_at(SELF_AT[ENDS[kind][0]])
        block_b = [from_next(column, by) for column in columns_at(SELF_AT[ENDS[kind][1]])]
        block_b = [shift_rows(column) for column in shift_columns(block_b)]
        for j in range(6):
            diagonal[j] = diagonal[j] + there * block_a[j] + to_next(there * block_b[j], by)
        pull_a = vector_at(PULL_AT[kind], 0)
        pull_b = shift_rows(vector_at(PULL_AT[kind], 1))
        load = load + there * pull_a + to_next(there * pull_b, by)
        coupling = [there * column for column in shift_columns(columns_at(PAIR_AT[kind]))]
        couplings.append((coupling, transposed_columns(coupling, sublane), by))

    inverse = inverse_columns(diagonal, sublane)

    def multiply(vector):
        result = apply_columns(diagonal, vector)
        for coupling, flipped, by in couplings:
            result = result + apply_columns(coupling, from_next(vector, by))
            result = result + to_next(apply_columns(flipped, vector), by)
        return result

    def total(array):
        return jnp.sum(jnp.sum(array, axis=0, keepdims=True), axis=1, keepdims=True)

    residual = load
    scaled = apply_columns(inverse, residual)
    product = multiply(scaled)
    rho_now, curve = total(residual * scaled), total(scaled * product)
    step_size = rho_now / curve
    direction, carried = scaled, product
    update = jnp.zeros_like(load)
    for step in range(ITERS):
        update = update + step_size * direction
        residual = residual - step_size * carried
        if step + 1 < ITERS:
            scaled = apply_columns(inverse, residual)
            product = multiply(scaled)
            rho_next, curve = total(residual * scaled), total(scaled * product)
            ratio = rho_next / rho_now
            step_size = rho_next / (curve - ratio * rho_next / step_size)
            direction = scaled + ratio * direction
            carried = product + ratio * carried
            rho_now = rho_next

    for out, values in ((update_ref, update), (residual_ref, residual)):
        for c in range(columns):
            own = jnp.sum(jnp.where(place == c * count + me, values, 0.0), axis=1, keepdims=True)
            out[:, c : c + 1] = own[0:6]

    pltpu.make_async_copy(others, others, gather_send).wait()
    for kind in range(2):

        @pl.when(sends[kind])
        def _():
            for c in range(columns):
                strip_copy(kind, c).wait_send()


def shards(tile_strips, pair_mask, strip_offset, stiffness):
    _, _, columns, images, height, width = tile_strips.shape
    sections = lax.axis_size("sec")
    tile_rows = lax.axis_size("tile")
    count = sections * tile_rows
    per_device = round_up(columns * QROWS, SUB)
    held = columns * (IMAGES + 2) * height
    out = jax.ShapeDtypeStruct((6, columns), jnp.float32)
    update, residual = pl.pallas_call(
        functools.partial(kernel, sections, tile_rows),
        out_shape=(out, out),
        in_specs=[
            pl.BlockSpec(memory_space=pl.ANY),
            pl.BlockSpec(memory_space=pltpu.SMEM),
            pl.BlockSpec(memory_space=pltpu.SMEM),
            pl.BlockSpec(memory_space=pltpu.SMEM),
        ],
        out_specs=(
            pl.BlockSpec(memory_space=pltpu.VMEM),
            pl.BlockSpec(memory_space=pltpu.VMEM),
        ),
        scratch_shapes=[
            pltpu.VMEM((columns, images, height, width), jnp.bfloat16),
            pltpu.VMEM((2, columns, height, width), jnp.bfloat16),
            pltpu.VMEM((held, width), jnp.float32),
            pltpu.VMEM((held, width), jnp.float32),
            pltpu.VMEM((columns * QROWS * LANES, LANES), jnp.float32),
            pltpu.VMEM((count * per_device, LANES), jnp.float32),
            pltpu.SemaphoreType.DMA,
            pltpu.SemaphoreType.DMA((2, columns)),
            pltpu.SemaphoreType.DMA((2, columns)),
            pltpu.SemaphoreType.DMA,
            pltpu.SemaphoreType.DMA,
        ],
        compiler_params=pltpu.CompilerParams(
            collective_id=0, has_side_effects=True, vmem_limit_bytes=32 * 1024 * 1024
        ),
    )(tile_strips[0, 0], pair_mask[0, 0], strip_offset[0, 0], stiffness[0, 0])
    shape = (6, 1, 1, columns)
    return update.reshape(shape), residual.reshape(shape)


def solution(mesh):
    return jax.shard_map(
        shards,
        mesh=mesh,
        in_specs=(
            P("sec", "tile", None, None, None, None),
            P("sec", "tile", None, None),
            P("sec", "tile", None, None, None),
            P("sec", "tile", None),
        ),
        out_specs=(P(None, "sec", "tile", None), P(None, "sec", "tile", None)),
        check_vma=False,
    )
```

time: 364 us -> 23.8 us (0.07)
  blocking collectives: 127 us -> 0 us
  local copies, waits for them, and re-layouts: 81.7 us -> 3.74 us
  starting transfers between devices: 53.2 us -> 0 us
  matrix products: 40.5 us -> 0 us
  other arithmetic: 33.7 us -> 0 us
  Pallas kernels: 0 us -> 19.2 us
  waiting for transfers between devices: 13.1 us -> 0 us
  between operations: 10.5 us -> 0.65 us
    psum x3 -> x0, blocking collectives: 127 us -> none  [paired_sum(): lax.psum((jnp.sum(residual * scaled), jnp.sum(scaled * product)), ('sec',...]
    ppermute x20 -> x0, starting transfers between devices: 53.2 us -> none  [the longest x8 24.2 us: passed_along(): return lax.ppermute(shard, axis, pairs)]
    dot_general x33 -> x0, matrix products: 40.5 us -> none  [the longest x6 17.1 us: pair_block(): jnp.dot(jacobian, jacobian.T, precision=highest, preferred_element_type=j...]
    while x118 -> x0, local copies, waits for them, and re-layouts: 32 us -> none
    concatenate x10 -> x0, local copies, waits for them, and re-layouts: 23.9 us -> none  [the longest x6 23.2 us: pair_block(): jnp.concatenate([jacobian_rows(first, zero, zero), -jacobian_rows(second,...]
    pallas_call x0 -> x1, Pallas kernels: none -> 19.2 us  [shards(): pl.pallas_call(functools.partial(kernel, sections, tile_rows), out_shape=...]
    ppermute x20 -> x0, waiting for transfers between devices: 13.1 us -> none  [the longest x6 11.5 us: with_halo(): lax.ppermute(head, axis, [((i + 1) % count, i) for i in range(ends)])]
    mul x30 -> x0, other arithmetic: 12.3 us -> none  [the longest x12 4.03 us: jacobian_rows(): along_x * coord_u]
  transfers between devices with their start and end apart: 20 -> 0, of which waited for: 7 -> 0; matrix products, arithmetic and copies ran while one was open for 39% -> 0% of each run, Pallas kernels for 0% -> 0%
where the time goes in v1:
time: 23.8 us; the launch traced here: 23.6 us
  Pallas kernels  19.2 us (81%)
  local copies, waits for them, and re-layouts  3.74 us (16%)
  between operations  0.65 us (3%)
    pallas_call x1, Pallas kernels, shards(): pl.pallas_call(functools.partial(kernel, sections, tile_rows), out_shape=...  19.2 us
    unnamed x8, local copies, waits for them, and re-layouts  2.34 us
    pallas_call x2, local copies, waits for them, and re-layouts, shards(): pl.pallas_call(functools.partial(kernel, sections, tile_rows), out_shape=...  1.3 us

profile of v1, /device:TPU:0, one launch (start us, length us, event | category | flops | bytes accessed | tf_op | source)
XLA Modules:
  0.0 23.6 jit_solution(7539105857775834098)
XLA Ops:
  0.6 0.0 copy-start.3
  0.6 0.7 %copy-done.3 = s32[1,1,2,3,2]{3,4,2,1,0:T(2,128)S(1)} copy-done((s32[1,1,2,3,2]{3,4,2,1,0:T(2,128)S(1)}, s32[1,1,2,3,2]{3,4,2,1,0:T(2,128)}, u32[]{:S(2)}) %copy-start.3) | copy-done | bytes 72
  1.3 0.0 copy-start.1
  1.3 0.0 copy-start.2
  1.3 0.1 copy.6.offset_ref
  1.4 0.6 %copy-done.1 = s32[1,1,2,3]{3,2,1,0:T(2,128)S(1)} copy-done((s32[1,1,2,3]{3,2,1,0:T(2,128)S(1)}, s32[1,1,2,3]{3,2,1,0:T(2,128)}, u32[]{:S(2)}) %copy-start.1) | copy-done | bytes 48
  2.0 0.0 copy-done.2
  2.0 0.0 copy-start
  2.0 1.1 %copy-done = bf16[1,1,2,5,64,512]{5,4,3,2,1,0:T(8,128)(2,1)S(1)} copy-done((bf16[1,1,2,5,64,512]{5,4,3,2,1,0:T(8,128)(2,1)S(1)}, bf16[1,1,2,5,64,512]{5,4,3,2,1,0:T(8,128)(2,1)}, u32[]{:S(2)}) %copy-start) | copy-done | bytes 655384
  3.1 19.2 %shard_map.59 = (f32[6,2]{1,0:T(8,128)S(1)}, f32[6,2]{1,0:T(8,128)S(1)}) custom-call(bf16[2,5,64,512]{3,2,1,0:T(8,128)(2,1)S(1)} %bitcast.6, s32[2,3]{1,0:T(2,128)S(1)} %bitcast.7, s32[2,3,2]{2,1,0:T(4,128)S(1)} %copy.6.offset_ref, f32[2]{0:T(128)S(1)} %bitcast.8), custom_call_target="tpu_custom_call" | custom-call | tf_op jit(solution)/shard_map/pallas_call | solution.py:454
  22.3 0.6 %copy.7 = f32[6,2]{0,1:T(2,128)} copy(f32[6,2]{1,0:T(8,128)S(1)} %get-tuple-element.4) | data formatting | bytes 96 | tf_op jit(solution)/shard_map/pallas_call | solution.py:454
  22.9 0.6 %copy.8 = f32[6,2]{0,1:T(2,128)} copy(f32[6,2]{1,0:T(8,128)S(1)} %get-tuple-element.5) | data formatting | bytes 96 | tf_op jit(solution)/shard_map/pallas_call | solution.py:454
Async XLA Ops:
  0.6 0.7 %copy-start.3 = (s32[1,1,2,3,2]{3,4,2,1,0:T(2,128)S(1)}, s32[1,1,2,3,2]{3,4,2,1,0:T(2,128)}, u32[]{:S(2)}) copy-start(s32[1,1,2,3,2]{3,4,2,1,0:T(2,128)} %param.6) | copy-start | bytes 148
  1.3 0.7 %copy-start.1 = (s32[1,1,2,3]{3,2,1,0:T(2,128)S(1)}, s32[1,1,2,3]{3,2,1,0:T(2,128)}, u32[]{:S(2)}) copy-start(s32[1,1,2,3]{3,2,1,0:T(2,128)} %param.5) | copy-start | bytes 76
  1.3 0.7 %copy-start.2 = (f32[1,1,2]{2,1,0:T(1,128)S(1)}, f32[1,1,2]{2,1,0:T(1,128)}, u32[]{:S(2)}) copy-start(f32[1,1,2]{2,1,0:T(1,128)} %param.7) | copy-start | bytes 28
  2.0 1.1 %copy-start = (bf16[1,1,2,5,64,512]{5,4,3,2,1,0:T(8,128)(2,1)S(1)}, bf16[1,1,2,5,64,512]{5,4,3,2,1,0:T(8,128)(2,1)}, u32[]{:S(2)}) copy-start(bf16[1,1,2,5,64,512]{5,4,3,2,1,0:T(8,128)(2,1)} %param.4) | copy-start | bytes 1966084

commit v2 on v1

v2 whole, which is shorter than its diff:
```python
import functools

import jax
import jax.numpy as jnp
from jax import lax
from jax.experimental import pallas as pl
from jax.experimental.pallas import tpu as pltpu
from jax.sharding import PartitionSpec as P

ITERS = 3
LANES = 128
SUB = 8
IMAGES = 5
KINDS = 3
QROWS = 2
MESH = pl.DeviceIdType.MESH

QUAD = 6
MOMENT = ((3, 4, 1), (4, 5, 2), (1, 2, 0))
SELF = 3 * QUAD
CROSS = 4 * QUAD
SUM_AT = 0
SELF_AT = (SELF, 2 * SELF, 3 * SELF)
OFFSET_AT = 96
EXISTS_AT = 102
STIFF_AT = 105
PAIR_AT = (LANES, LANES + CROSS, LANES + 2 * CROSS)
PULL_A_AT = LANES + 3 * CROSS
PULL_B_AT = PULL_A_AT + 6
ENDS = ((1, 0), (3, 2), (4, 4))


def round_up(value, unit):
    return (value + unit - 1) // unit * unit


def column_moments(fields, width, quadratic):
    groups = fields.groups
    sums = None
    for k in range(groups):
        values = fields(k)
        if sums is None:
            sums = [[value] * (3 if quadratic else 2) for value in values]
        else:
            for entry, value in zip(sums, values):
                entry[0] = entry[0] + value
                entry[1] = entry[1] + entry[0]
                if quadratic:
                    entry[2] = entry[2] + entry[1]
    height = groups * SUB
    step = SUB / height
    row = lax.broadcasted_iota(jnp.int32, (SUB, width), 0).astype(jnp.float32)
    column = lax.broadcasted_iota(jnp.int32, (SUB, width), 1).astype(jnp.float32)
    edge = row / height + 0.5
    u = column / width - 0.5

    def fold(array):
        total = array[:, :LANES]
        for start in range(LANES, width, LANES):
            total = total + array[:, start : start + LANES]
        return jnp.sum(total, axis=0, keepdims=True)

    out = []
    for entry in sums:
        zeroth = entry[0]
        first = edge * zeroth - step * entry[1]
        scaled = u * zeroth
        moments = [fold(zeroth), fold(scaled), fold(first)]
        if quadratic:
            second = (
                edge * edge * zeroth
                - (2.0 * step) * edge * entry[1]
                + (step * step) * (2.0 * entry[2] - entry[1])
            )
            moments += [fold(u * scaled), fold(u * first), fold(second)]
        out.append(moments)
    return out


class Products:
    def __init__(self, groups, form):
        self.groups = groups
        self.form = form

    def __call__(self, k):
        return self.form(k)


def apply_columns(columns, vector):
    total = columns[0] * vector[0:1]
    for j in range(1, 6):
        total = total + columns[j] * vector[j : j + 1]
    return total


def inverse_columns(columns, sublane):
    columns = list(columns)
    for p in range(6):
        pivot = 1.0 / columns[p][p : p + 1]
        here = sublane == p
        lead = columns[p]
        for j in range(6):
            if j != p:
                ratio = columns[j][p : p + 1] * pivot
                columns[j] = jnp.where(here, ratio, columns[j] - lead * ratio)
        columns[p] = jnp.where(here, pivot, -lead * pivot)
    return columns


def transposed_columns(columns, sublane):
    out = []
    for i in range(6):
        total = jnp.zeros_like(columns[0])
        for j in range(6):
            total = jnp.where(sublane == j, columns[j][i : i + 1], total)
        out.append(total)
    return out


def kernel(
    sections,
    tile_rows,
    strips_hbm,
    mask_hbm,
    offset_hbm,
    stiff_hbm,
    out_ref,
    strips,
    landed,
    grad_x,
    grad_y,
    rows,
    gathered,
    table,
    mask_ref,
    offset_ref,
    stiff_ref,
    local_sem,
    strip_send,
    strip_recv,
    gather_send,
    gather_recv,
):
    columns, _, height, width = strips.shape
    count = sections * tile_rows
    per_device = gathered.shape[0] // count
    used = columns * QROWS
    groups = height // SUB
    own_images = columns * IMAGES
    section = lax.axis_index("sec")
    tile_row = lax.axis_index("tile")
    me = section * tile_rows + tile_row

    def device(step):
        other = lax.rem(me + step, count)
        return (other // tile_rows, lax.rem(other, tile_rows))

    barrier = pltpu.get_barrier_semaphore()

    @pl.loop(1, count)
    def _(step):
        pl.semaphore_signal(barrier, inc=1, device_id=device(step), device_id_type=MESH)

    local = [
        pltpu.make_async_copy(source, target, local_sem.at[index])
        for index, (source, target) in enumerate(
            (
                (strips_hbm, strips),
                (mask_hbm, mask_ref),
                (offset_hbm, offset_ref),
                (stiff_hbm, stiff_ref),
            )
        )
    ]
    for copy in local:
        copy.start()

    first = lax.broadcasted_iota(jnp.int32, (height, height), 0)
    second = lax.broadcasted_iota(jnp.int32, (height, height), 1)
    gap = second - first
    down = jnp.where(gap == 1, 0.5, jnp.where(gap == -1, -0.5, 0.0)).astype(jnp.bfloat16)
    rows[...] = jnp.zeros_like(rows)

    pl.semaphore_wait(barrier, count - 1)

    def strip_copy(kind, c):
        target = (section, tile_row - 1) if kind == 0 else (section - 1, tile_row)
        return pltpu.make_async_remote_copy(
            src_ref=strips_hbm.at[c, 2 if kind == 0 else 4],
            dst_ref=landed.at[kind, c],
            send_sem=strip_send.at[kind, c],
            recv_sem=strip_recv.at[kind, c],
            device_id=target,
            device_id_type=MESH,
        )

    sends = (tile_row > 0, section > 0)
    receives = (tile_row < tile_rows - 1, section < sections - 1)
    for kind in range(2):

        @pl.when(sends[kind])
        def _():
            for c in range(columns):
                strip_copy(kind, c).start()

    for copy in local:
        copy.wait()

    column = lax.broadcasted_iota(jnp.int32, (height, width), 1)

    def gradients(image, at):
        values = image.astype(jnp.float32)
        before = jnp.where(column == 0, 0.0, pltpu.roll(values, 1, 1))
        after = jnp.where(column == width - 1, 0.0, pltpu.roll(values, width - 1, 1))
        spot = pl.ds(pl.multiple_of(at * height, SUB), height)
        grad_x[spot, :] = (after - before) * 0.5
        grad_y[spot, :] = jnp.dot(down, image, preferred_element_type=jnp.float32)

    def group(ref, image, k):
        return ref[pl.ds(pl.multiple_of(image * height + k * SUB, SUB), SUB), :]

    def put(row, value):
        rows[pl.ds(row, 1), :] = value

    def add(row, value):
        rows[pl.ds(row, 1), :] = rows[pl.ds(row, 1), :] + value

    def exists(c, kind):
        inside = (jnp.int32(c) < columns - 1, receives[0], receives[1])[kind]
        return jnp.where((mask_ref[c, kind] == 1) & inside, 1.0, 0.0)

    def self_blocks(c, image, a_kind, b_kind):
        at = c * IMAGES + image
        gradients(strips[c, image], at)

        def form(k):
            x, y = group(grad_x, at, k), group(grad_y, at, k)
            return (x * x, x * y, y * y)

        base = c * (QROWS * LANES)
        for index, entry in enumerate(column_moments(Products(groups, form), width, True)):
            for moment, value in enumerate(entry):
                spot = index * QUAD + moment
                if a_kind is not None:
                    add(base + SUM_AT + spot, exists(c, a_kind) * value)
                if b_kind is not None:
                    put(base + SELF_AT[b_kind] + spot, value)

    def pair_blocks(kind, c, at_a, at_b, image_a, image_b):
        there = exists(c, kind)
        base = c * (QROWS * LANES)
        for p, ref in enumerate((grad_x, grad_y)):

            def cross(k):
                value = group(ref, at_a, k)
                return (value * group(grad_x, at_b, k), value * group(grad_y, at_b, k))

            for q, entry in enumerate(column_moments(Products(groups, cross), width, True)):
                for moment, value in enumerate(entry):
                    put(base + PAIR_AT[kind] + (2 * p + q) * QUAD + moment, -there * value)

        misfit = image_a.astype(jnp.float32) - image_b.astype(jnp.float32)

        def pulls(k):
            miss = misfit[k * SUB : (k + 1) * SUB]
            return (
                group(grad_x, at_a, k) * miss,
                group(grad_y, at_a, k) * miss,
                group(grad_x, at_b, k) * miss,
                group(grad_y, at_b, k) * miss,
            )

        for index, entry in enumerate(column_moments(Products(groups, pulls), width, False)):
            side, p = divmod(index, 2)
            for weight, value in zip((2, 0, 1), entry):
                if side:
                    put(base + PULL_B_AT + 6 * kind + 3 * p + weight, there * value)
                else:
                    add(base + PULL_A_AT + 3 * p + weight, -there * value)

    @pl.loop(0, columns)
    def _(c):
        self_blocks(c, 4, 2, 2)
        self_blocks(c, 3, 1, None)
        self_blocks(c, 2, None, 1)

    @pl.loop(0, columns - 1)
    def _(c):
        self_blocks(c, 1, 0, None)
        self_blocks(c + 1, 0, None, 0)
        pair_blocks(0, c, c * IMAGES + 1, (c + 1) * IMAGES, strips[c, 1], strips[c + 1, 0])

    ones = jnp.ones((SUB, LANES), jnp.bfloat16)
    lane = lax.broadcasted_iota(jnp.int32, (1, LANES), 1)
    contract = (((1,), (1,)), ((), ()))
    mine = pl.multiple_of(me * per_device, SUB)

    def line_of(c, h):
        part = rows[(c * QROWS + h) * LANES : (c * QROWS + h + 1) * LANES, :]
        high = part.astype(jnp.bfloat16)
        low = (part - high.astype(jnp.float32)).astype(jnp.bfloat16)
        summed = lax.dot_general(ones, high, contract, preferred_element_type=jnp.float32)
        summed = summed + lax.dot_general(ones, low, contract, preferred_element_type=jnp.float32)
        return summed[0:1] * (1.0 / (height * width))

    for c in range(columns):
        line = line_of(c, 0)
        for kind in range(KINDS):
            for axis, extent in ((0, width), (1, height)):
                shift = offset_ref[c, axis, kind].astype(jnp.float32) / extent
                line = jnp.where(lane == OFFSET_AT + 2 * kind + axis, shift, line)
            line = jnp.where(lane == EXISTS_AT + kind, exists(c, kind), line)
        line = jnp.where(lane == STIFF_AT, stiff_ref[c], line)
        gathered[pl.ds(mine + c * QROWS, 1), :] = line

    for kind in (1, 0):

        @pl.when(receives[kind])
        def _():
            @pl.loop(0, columns)
            def _(c):
                strip_copy(kind, c).wait_recv()
                image = ENDS[kind + 1][0]
                at_b = own_images + kind * columns + c
                gradients(landed[kind, c], at_b)
                pair_blocks(
                    kind + 1, c, c * IMAGES + image, at_b, strips[c, image], landed[kind, c]
                )

    for c in range(columns):
        gathered[pl.ds(mine + c * QROWS + 1, 1), :] = line_of(c, 1)

    @pl.loop(1, count)
    def _(step):
        pltpu.make_async_remote_copy(
            src_ref=gathered.at[pl.ds(mine, used)],
            dst_ref=gathered.at[pl.ds(mine, used)],
            send_sem=gather_send,
            recv_sem=gather_recv,
            device_id=device(step),
            device_id_type=MESH,
        ).start()

    others = gathered.at[pl.ds(0, (count - 1) * used)]
    pltpu.make_async_copy(others, others, gather_recv).wait()

    tiles = columns * count
    padded = round_up(tiles, LANES)
    for h in range(QROWS):
        parts = [
            gathered[pl.ds(c * QROWS + h, count, stride=per_device), :] for c in range(columns)
        ]
        if padded > tiles:
            parts.append(jnp.zeros((padded - tiles, LANES), jnp.float32))
        table[h * LANES : (h + 1) * LANES, :] = jnp.concatenate(parts, axis=0).T

    sublane = lax.broadcasted_iota(jnp.int32, (SUB, padded), 0)
    place = lax.broadcasted_iota(jnp.int32, (SUB, padded), 1)
    picks = [sublane == i for i in range(6)]

    def entry(at):
        return table[at : at + 1, :]

    def stacked(spots):
        total = jnp.zeros((SUB, padded), jnp.float32)
        for pick, at in zip(picks, spots):
            total = jnp.where(pick, entry(at), total)
        return total

    def block_at(base, field):
        return [
            stacked(
                [base + field[p][q] * QUAD + MOMENT[a][b] for p in range(2) for a in range(3)]
            )
            for q in range(2)
            for b in range(3)
        ]

    own_field = ((0, 1), (1, 2))
    pair_field = ((0, 1), (2, 3))

    def to_next(array, by):
        return pltpu.roll(array, by, 1)

    def from_next(array, by):
        return pltpu.roll(array, padded - by, 1)

    def shift_rows(vector, offset):
        return vector + offset * jnp.where(sublane < 3, vector[2:3], vector[5:6])

    def shift_columns(block, offset):
        du, dv = offset[0:1], offset[1:2]
        out = []
        for p in range(2):
            last = block[3 * p + 2]
            out += [block[3 * p] + du * last, block[3 * p + 1] + dv * last, last]
        return out

    shifts = (count, 1, tile_rows)
    stiffness = jnp.where(place < tiles, entry(STIFF_AT), 1.0)
    diagonal = [
        column + jnp.where(pick, stiffness, 0.0)
        for pick, column in zip(picks, block_at(SUM_AT, own_field))
    ]
    load = stacked([PULL_A_AT + i for i in range(6)])
    couplings = []
    for kind in range(KINDS):
        by = shifts[kind]
        du, dv = entry(OFFSET_AT + 2 * kind), entry(OFFSET_AT + 2 * kind + 1)
        offset = jnp.where(picks[0] | picks[3], du, jnp.where(picks[1] | picks[4], dv, 0.0))
        offset_b = to_next(offset, by)
        there_b = to_next(jnp.broadcast_to(entry(EXISTS_AT + kind), offset.shape), by)
        block_b = shift_columns(block_at(SELF_AT[kind], own_field), offset_b)
        for j in range(6):
            diagonal[j] = diagonal[j] + there_b * shift_rows(block_b[j], offset_b)
        pull_b = stacked([PULL_B_AT + 6 * kind + i for i in range(6)])
        load = load + to_next(shift_rows(pull_b, offset), by)
        coupling = shift_columns(block_at(PAIR_AT[kind], pair_field), offset)
        couplings.append((coupling, transposed_columns(coupling, sublane), by))

    inverse = inverse_columns(diagonal, sublane)

    def multiply(vector):
        result = apply_columns(diagonal, vector)
        for coupling, flipped, by in couplings:
            result = result + apply_columns(coupling, from_next(vector, by))
            result = result + to_next(apply_columns(flipped, vector), by)
        return result

    def total(array):
        return jnp.sum(jnp.sum(array, axis=0, keepdims=True), axis=1, keepdims=True)

    residual = load
    scaled = apply_columns(inverse, residual)
    product = multiply(scaled)
    rho_now, curve = total(residual * scaled), total(scaled * product)
    step_size = rho_now / curve
    direction, carried = scaled, product
    update = jnp.zeros_like(load)
    for step in range(ITERS):
        update = update + step_size * direction
        residual = residual - step_size * carried
        if step + 1 < ITERS:
            scaled = apply_columns(inverse, residual)
            product = multiply(scaled)
            rho_next, curve = total(residual * scaled), total(scaled * product)
            ratio = rho_next / rho_now
            step_size = rho_next / (curve - ratio * rho_next / step_size)
            direction = scaled + ratio * direction
            carried = product + ratio * carried
            rho_now = rho_next

    turn = sublane[:, :LANES] == place[:, :LANES]
    for index, values in enumerate((update, residual)):
        for c in range(columns):
            own = jnp.sum(jnp.where(place == c * count + me, values, 0.0), axis=1, keepdims=True)
            line = jnp.sum(jnp.where(turn, own, 0.0), axis=0, keepdims=True)
            out_ref[index, c : c + 1, :] = line[:, 0:6]

    pltpu.make_async_copy(others, others, gather_send).wait()
    for kind in range(2):

        @pl.when(sends[kind])
        def _():
            for c in range(columns):
                strip_copy(kind, c).wait_send()


def shards(tile_strips, pair_mask, strip_offset, stiffness):
    _, _, columns, images, height, width = tile_strips.shape
    sections = lax.axis_size("sec")
    tile_rows = lax.axis_size("tile")
    count = sections * tile_rows
    per_device = round_up(columns * QROWS, SUB)
    held = columns * (IMAGES + 2) * height
    padded = round_up(columns * count, LANES)
    both = pl.pallas_call(
        functools.partial(kernel, sections, tile_rows),
        out_shape=jax.ShapeDtypeStruct((2, columns, 6), jnp.float32),
        in_specs=[pl.BlockSpec(memory_space=pltpu.HBM)] * 4,
        out_specs=pl.BlockSpec(memory_space=pltpu.VMEM),
        scratch_shapes=[
            pltpu.VMEM((columns, images, height, width), jnp.bfloat16),
            pltpu.VMEM((2, columns, height, width), jnp.bfloat16),
            pltpu.VMEM((held, width), jnp.float32),
            pltpu.VMEM((held, width), jnp.float32),
            pltpu.VMEM((columns * QROWS * LANES, LANES), jnp.float32),
            pltpu.VMEM((count * per_device, LANES), jnp.float32),
            pltpu.VMEM((QROWS * LANES, padded), jnp.float32),
            pltpu.SMEM((columns, KINDS), jnp.int32),
            pltpu.SMEM((columns, 2, KINDS), jnp.int32),
            pltpu.SMEM((columns,), jnp.float32),
            pltpu.SemaphoreType.DMA((4,)),
            pltpu.SemaphoreType.DMA((2, columns)),
            pltpu.SemaphoreType.DMA((2, columns)),
            pltpu.SemaphoreType.DMA,
            pltpu.SemaphoreType.DMA,
        ],
        compiler_params=pltpu.CompilerParams(
            collective_id=0, has_side_effects=True, vmem_limit_bytes=60 * 1024 * 1024
        ),
    )(
        tile_strips[0, 0],
        pair_mask[0, 0],
        jnp.swapaxes(strip_offset[0, 0], 1, 2),
        stiffness[0, 0],
    )
    both = jnp.swapaxes(both, 1, 2).reshape(2, 6, 1, 1, columns)
    return both[0], both[1]


def solution(mesh):
    return jax.shard_map(
        shards,
        mesh=mesh,
        in_specs=(
            P("sec", "tile", None, None, None, None),
            P("sec", "tile", None, None),
            P("sec", "tile", None, None, None),
            P("sec", "tile", None),
        ),
        out_specs=(P(None, "sec", "tile", None), P(None, "sec", "tile", None)),
        check_vma=False,
    )
```

time: 23.8 us -> 19.8 us (0.83)
  local copies, waits for them, and re-layouts: 3.74 us -> 1.24 us
  Pallas kernels: 19.2 us -> 17.7 us
    unnamed x8 -> x0, local copies, waits for them, and re-layouts: 2.34 us -> none
    pallas_call x1, Pallas kernels: 19.2 us -> 17.7 us  [shards(): pl.pallas_call(functools.partial(kernel, sections, tile_rows), out_shape=...]
    pallas_call x2 -> x0, local copies, waits for them, and re-layouts: 1.3 us -> none  [shards(): pl.pallas_call(functools.partial(kernel, sections, tile_rows), out_shape=...]
    squeeze x1, local copies, waits for them, and re-layouts: 0.1 us -> 1.24 us  [shards(): return (both[0], both[1])]
where the time goes in v2:
time: 19.8 us; the launch traced here: 19.6 us
  Pallas kernels  17.7 us (89%)
  local copies, waits for them, and re-layouts  1.24 us (6%)
  between operations  0.64 us (3%)
    pallas_call x1, Pallas kernels, shards(): pl.pallas_call(functools.partial(kernel, sections, tile_rows), out_shape=...  17.7 us
    squeeze x1, local copies, waits for them, and re-layouts, shards(): return (both[0], both[1])  1.24 us

profile of v2, /device:TPU:0, one launch (start us, length us, event | category | flops | bytes accessed | tf_op | source)
XLA Modules:
  0.0 19.6 jit_solution(13827754960403304101)
XLA Ops:
  0.6 17.7 %shard_map.59 = f32[2,2,6]{2,1,0:T(2,128)} custom-call(bf16[2,5,64,512]{3,2,1,0:T(8,128)(2,1)} %bitcast.11, s32[2,3]{1,0:T(2,128)} %bitcast.14, s32[2,2,3]{2,1,0:T(2,128)} %bitcast.13, f32[2]{0:T(128)} %bitcast.15), custom_call_target="tpu_custom_call" | custom-call | tf_op jit(solution)/shard_map/pallas_call | solution.py:477
  18.4 1.2 %slice_bitcast_fusion = (f32[6,1,1,2]{0,3,2,1:T(2,128)}, f32[6,1,1,2]{0,3,2,1:T(2,128)}) fusion(f32[2,6,2]{1,2,0:T(2,128)} %bitcast.12), kind=kLoop, calls=%fused_computation | loop fusion | bytes 192 | tf_op jit(solution)/shard_map/squeeze | solution.py:509

commit v3 on v2

--- a/solution.py
+++ b/solution.py
@@ -49,7 +49,7 @@
                     entry[2] = entry[2] + entry[1]
     height = groups * SUB
     step = SUB / height
-    row = lax.broadcasted_iota(jnp.int32, (SUB, width), 0).astype(jnp.float32)
+    row = lax.broadcasted_iota(jnp.int32, (SUB, LANES), 0).astype(jnp.float32)
     column = lax.broadcasted_iota(jnp.int32, (SUB, width), 1).astype(jnp.float32)
     edge = row / height + 0.5
     u = column / width - 0.5
@@ -58,22 +58,22 @@
         total = array[:, :LANES]
         for start in range(LANES, width, LANES):
             total = total + array[:, start : start + LANES]
-        return jnp.sum(total, axis=0, keepdims=True)
+        return total
 
     out = []
     for entry in sums:
-        zeroth = entry[0]
-        first = edge * zeroth - step * entry[1]
-        scaled = u * zeroth
-        moments = [fold(zeroth), fold(scaled), fold(first)]
+        first, second = fold(entry[0]), fold(entry[1])
+        scaled = u * entry[0]
+        along = fold(scaled)
+        moments = [first, along, edge * first - step * second]
         if quadratic:
-            second = (
-                edge * edge * zeroth
-                - (2.0 * step) * edge * entry[1]
-                + (step * step) * (2.0 * entry[2] - entry[1])
-            )
-            moments += [fold(u * scaled), fold(u * first), fold(second)]
-        out.append(moments)
+            third = 2.0 * fold(entry[2]) - second
+            moments += [
+                fold(u * scaled),
+                edge * along - step * fold(u * entry[1]),
+                edge * (edge * first - (2.0 * step) * second) + (step * step) * third,
+            ]
+        out.append([jnp.sum(moment, axis=0, keepdims=True) for moment in moments])
     return out
 
 

time: 19.8 us -> 19.7 us (level)
  no operation moved by 1% of the time
where the time goes in v3:
time: 19.7 us; the launch traced here: 19.6 us
  Pallas kernels  17.7 us (90%)
  local copies, waits for them, and re-layouts  1.24 us (6%)
  between operations  0.64 us (3%)
    pallas_call x1, Pallas kernels, shards(): pl.pallas_call(functools.partial(kernel, sections, tile_rows), out_shape=...  17.7 us
    squeeze x1, local copies, waits for them, and re-layouts, shards(): return (both[0], both[1])  1.24 us

profile of v3, /device:TPU:0, one launch (start us, length us, event | category | flops | bytes accessed | tf_op | source)
XLA Modules:
  0.0 19.6 jit_solution(14078105480763773775)
XLA Ops:
  0.6 17.7 %shard_map.59 = f32[2,2,6]{2,1,0:T(2,128)} custom-call(bf16[2,5,64,512]{3,2,1,0:T(8,128)(2,1)} %bitcast.11, s32[2,3]{1,0:T(2,128)} %bitcast.14, s32[2,2,3]{2,1,0:T(2,128)} %bitcast.13, f32[2]{0:T(128)} %bitcast.15), custom_call_target="tpu_custom_call" | custom-call | tf_op jit(solution)/shard_map/pallas_call | solution.py:477
  18.3 1.2 %slice_bitcast_fusion = (f32[6,1,1,2]{0,3,2,1:T(2,128)}, f32[6,1,1,2]{0,3,2,1:T(2,128)}) fusion(f32[2,6,2]{1,2,0:T(2,128)} %bitcast.12), kind=kLoop, calls=%fused_computation | loop fusion | bytes 192 | tf_op jit(solution)/shard_map/squeeze | solution.py:509

commit v4 on v3

--- a/solution.py
+++ b/solution.py
@@ -143,7 +143,6 @@
 ):
     columns, _, height, width = strips.shape
     count = sections * tile_rows
-    per_device = gathered.shape[0] // count
     used = columns * QROWS
     groups = height // SUB
     own_images = columns * IMAGES
@@ -151,15 +150,19 @@
     tile_row = lax.axis_index("tile")
     me = section * tile_rows + tile_row
 
-    def device(step):
-        other = lax.rem(me + step, count)
-        return (other // tile_rows, lax.rem(other, tile_rows))
+    def along_tile(step):
+        return (section, lax.rem(tile_row + step, tile_rows))
+
+    def along_sec(step):
+        return (lax.rem(section + step, sections), tile_row)
 
     barrier = pltpu.get_barrier_semaphore()
 
-    @pl.loop(1, count)
-    def _(step):
-        pl.semaphore_signal(barrier, inc=1, device_id=device(step), device_id_type=MESH)
+    for size, device in ((tile_rows, along_tile), (sections, along_sec)):
+
+        @pl.loop(1, size)
+        def _(step):
+            pl.semaphore_signal(barrier, inc=1, device_id=device(step), device_id_type=MESH)
 
     local = [
         pltpu.make_async_copy(source, target, local_sem.at[index])
@@ -181,7 +184,7 @@
     down = jnp.where(gap == 1, 0.5, jnp.where(gap == -1, -0.5, 0.0)).astype(jnp.bfloat16)
     rows[...] = jnp.zeros_like(rows)
 
-    pl.semaphore_wait(barrier, count - 1)
+    pl.semaphore_wait(barrier, tile_rows + sections - 2)
 
     def strip_copy(kind, c):
         target = (section, tile_row - 1) if kind == 0 else (section - 1, tile_row)
@@ -293,7 +296,6 @@
     ones = jnp.ones((SUB, LANES), jnp.bfloat16)
     lane = lax.broadcasted_iota(jnp.int32, (1, LANES), 1)
     contract = (((1,), (1,)), ((), ()))
-    mine = pl.multiple_of(me * per_device, SUB)
 
     def line_of(c, h):
         part = rows[(c * QROWS + h) * LANES : (c * QROWS + h + 1) * LANES, :]
@@ -311,7 +313,7 @@
                 line = jnp.where(lane == OFFSET_AT + 2 * kind + axis, shift, line)
             line = jnp.where(lane == EXISTS_AT + kind, exists(c, kind), line)
         line = jnp.where(lane == STIFF_AT, stiff_ref[c], line)
-        gathered[pl.ds(mine + c * QROWS, 1), :] = line
+        gathered[me, c * QROWS : c * QROWS + 1, :] = line
 
     for kind in (1, 0):
 
@@ -328,27 +330,36 @@
                 )
 
     for c in range(columns):
-        gathered[pl.ds(mine + c * QROWS + 1, 1), :] = line_of(c, 1)
-
-    @pl.loop(1, count)
-    def _(step):
-        pltpu.make_async_remote_copy(
-            src_ref=gathered.at[pl.ds(mine, used)],
-            dst_ref=gathered.at[pl.ds(mine, used)],
-            send_sem=gather_send,
-            recv_sem=gather_recv,
-            device_id=device(step),
-            device_id_type=MESH,
-        ).start()
-
-    others = gathered.at[pl.ds(0, (count - 1) * used)]
-    pltpu.make_async_copy(others, others, gather_recv).wait()
+        gathered[me, c * QROWS + 1 : c * QROWS + 2, :] = line_of(c, 1)
+
+    def slots(start, length):
+        return gathered.at[pl.ds(start, length), pl.ds(0, used)]
+
+    stages = (
+        (tile_rows, along_tile, me, 1),
+        (sections, along_sec, section * tile_rows, tile_rows),
+    )
+    for stage, (size, device, start, length) in enumerate(stages):
+
+        @pl.loop(1, size)
+        def _(step):
+            pltpu.make_async_remote_copy(
+                src_ref=slots(start, length),
+                dst_ref=slots(start, length),
+                send_sem=gather_send.at[stage],
+                recv_sem=gather_recv.at[stage],
+                device_id=device(step),
+                device_id_type=MESH,
+            ).start()
+
+        others = slots(0, (size - 1) * length)
+        pltpu.make_async_copy(others, others, gather_recv.at[stage]).wait()
 
     tiles = columns * count
     padded = round_up(tiles, LANES)
     for h in range(QROWS):
         parts = [
-            gathered[pl.ds(c * QROWS + h, count, stride=per_device), :] for c in range(columns)
+            gathered[:, c * QROWS + h, :] for c in range(columns)
         ]
         if padded > tiles:
             parts.append(jnp.zeros((padded - tiles, LANES), jnp.float32))
@@ -457,7 +468,9 @@
             line = jnp.sum(jnp.where(turn, own, 0.0), axis=0, keepdims=True)
             out_ref[index, c : c + 1, :] = line[:, 0:6]
 
-    pltpu.make_async_copy(others, others, gather_send).wait()
+    for stage, (size, _, _, length) in enumerate(stages):
+        others = slots(0, (size - 1) * length)
+        pltpu.make_async_copy(others, others, gather_send.at[stage]).wait()
     for kind in range(2):
 
         @pl.when(sends[kind])
@@ -485,7 +498,7 @@
             pltpu.VMEM((held, width), jnp.float32),
             pltpu.VMEM((held, width), jnp.float32),
             pltpu.VMEM((columns * QROWS * LANES, LANES), jnp.float32),
-            pltpu.VMEM((count * per_device, LANES), jnp.float32),
+            pltpu.VMEM((count, per_device, LANES), jnp.float32),
             pltpu.VMEM((QROWS * LANES, padded), jnp.float32),
             pltpu.SMEM((columns, KINDS), jnp.int32),
             pltpu.SMEM((columns, 2, KINDS), jnp.int32),
@@ -493,11 +506,11 @@
             pltpu.SemaphoreType.DMA((4,)),
             pltpu.SemaphoreType.DMA((2, columns)),
             pltpu.SemaphoreType.DMA((2, columns)),
-            pltpu.SemaphoreType.DMA,
-            pltpu.SemaphoreType.DMA,
+            pltpu.SemaphoreType.DMA((2,)),
+            pltpu.SemaphoreType.DMA((2,)),
         ],
         compiler_params=pltpu.CompilerParams(
-            collective_id=0, has_side_effects=True, vmem_limit_bytes=60 * 1024 * 1024
+            collective_id=0, has_side_effects=True, vmem_limit_bytes=54784 * 1024
         ),
     )(
         tile_strips[0, 0],

time: 19.7 us -> 19.9 us (1.010)
  Pallas kernels: 17.7 us -> 17.9 us
    unnamed x0 -> x6, local copies, waits for them, and re-layouts: none -> 0.67 us
    squeeze x1, local copies, waits for them, and re-layouts: 1.24 us -> 0.57 us  [shards(): return (both[0], both[1])]
where the time goes in v4:
time: 19.9 us; the launch traced here: 19.8 us
  Pallas kernels  17.9 us (90%)
  local copies, waits for them, and re-layouts  1.24 us (6%)
  between operations  0.66 us (3%)
    pallas_call x1, Pallas kernels, shards(): pl.pallas_call(functools.partial(kernel, sections, tile_rows), out_shape=...  17.9 us
    unnamed x6, local copies, waits for them, and re-layouts  0.67 us
    squeeze x1, local copies, waits for them, and re-layouts, shards(): return (both[0], both[1])  0.57 us

profile of v4, /device:TPU:0, one launch (start us, length us, event | category | flops | bytes accessed | tf_op | source)
XLA Modules:
  0.0 19.8 jit_solution(3669574645678655943)
XLA Ops:
  0.6 0.0 copy-start
  0.6 0.0 copy-start.1
  0.7 0.0 copy-start.2
  0.7 0.7 %copy-done = s32[1,1,2,3,2]{3,4,2,1,0:T(2,128)S(1)} copy-done((s32[1,1,2,3,2]{3,4,2,1,0:T(2,128)S(1)}, s32[1,1,2,3,2]{3,4,2,1,0:T(2,128)}, u32[]{:S(2)}) %copy-start) | copy-done | bytes 72
  1.3 0.0 copy-done.1
  1.3 0.0 copy-done.2
  1.3 17.9 %shard_map.59 = f32[2,2,6]{2,1,0:T(2,128)S(1)} custom-call(bf16[2,5,64,512]{3,2,1,0:T(8,128)(2,1)} %bitcast.15, s32[2,3]{1,0:T(2,128)S(1)} %bitcast.13, s32[2,2,3]{2,1,0:T(2,128)S(1)} %bitcast.12, f32[2]{0:T(128)S(1)} %bitcast.14), custom_call_target="tpu_custom_call" | custom-call | tf_op jit(solution)/shard_map/pallas_call | solution.py:490
  19.2 0.6 %slice_bitcast_fusion = (f32[6,1,1,2]{0,3,2,1:T(2,128)}, f32[6,1,1,2]{0,3,2,1:T(2,128)}) fusion(f32[2,6,2]{1,2,0:T(2,128)S(1)} %bitcast.11), kind=kLoop, calls=%fused_computation | loop fusion | bytes 192 | tf_op jit(solution)/shard_map/squeeze | solution.py:522
Async XLA Ops:
  0.6 0.7 %copy-start = (s32[1,1,2,3,2]{3,4,2,1,0:T(2,128)S(1)}, s32[1,1,2,3,2]{3,4,2,1,0:T(2,128)}, u32[]{:S(2)}) copy-start(s32[1,1,2,3,2]{3,4,2,1,0:T(2,128)} %param.6) | copy-start | bytes 148
  0.6 0.7 %copy-start.1 = (s32[1,1,2,3]{3,2,1,0:T(2,128)S(1)}, s32[1,1,2,3]{3,2,1,0:T(2,128)}, u32[]{:S(2)}) copy-start(s32[1,1,2,3]{3,2,1,0:T(2,128)} %param.5) | copy-start | bytes 76
  0.7 0.7 %copy-start.2 = (f32[1,1,2]{2,1,0:T(1,128)S(1)}, f32[1,1,2]{2,1,0:T(1,128)}, u32[]{:S(2)}) copy-start(f32[1,1,2]{2,1,0:T(1,128)} %param.7) | copy-start | bytes 28

commit v5 on v3

--- a/solution.py
+++ b/solution.py
@@ -130,7 +130,8 @@
     grad_x,
     grad_y,
     rows,
-    gathered,
+    early,
+    late,
     table,
     mask_ref,
     offset_ref,
@@ -143,8 +144,7 @@
 ):
     columns, _, height, width = strips.shape
     count = sections * tile_rows
-    per_device = gathered.shape[0] // count
-    used = columns * QROWS
+    per_device = early.shape[0] // count
     groups = height // SUB
     own_images = columns * IMAGES
     section = lax.axis_index("sec")
@@ -311,7 +311,25 @@
                 line = jnp.where(lane == OFFSET_AT + 2 * kind + axis, shift, line)
             line = jnp.where(lane == EXISTS_AT + kind, exists(c, kind), line)
         line = jnp.where(lane == STIFF_AT, stiff_ref[c], line)
-        gathered[pl.ds(mine + c * QROWS, 1), :] = line
+        early[pl.ds(mine + c, 1), :] = line
+
+    def send_all(ref, stage):
+        @pl.loop(1, count)
+        def _(step):
+            pltpu.make_async_remote_copy(
+                src_ref=ref.at[pl.ds(mine, columns)],
+                dst_ref=ref.at[pl.ds(mine, columns)],
+                send_sem=gather_send.at[stage],
+                recv_sem=gather_recv.at[stage],
+                device_id=device(step),
+                device_id_type=MESH,
+            ).start()
+
+    def wait_all(ref, sem):
+        others = ref.at[pl.ds(0, (count - 1) * columns)]
+        pltpu.make_async_copy(others, others, sem).wait()
+
+    send_all(early, 0)
 
     for kind in (1, 0):
 
@@ -328,31 +346,21 @@
                 )
 
     for c in range(columns):
-        gathered[pl.ds(mine + c * QROWS + 1, 1), :] = line_of(c, 1)
-
-    @pl.loop(1, count)
-    def _(step):
-        pltpu.make_async_remote_copy(
-            src_ref=gathered.at[pl.ds(mine, used)],
-            dst_ref=gathered.at[pl.ds(mine, used)],
-            send_sem=gather_send,
-            recv_sem=gather_recv,
-            device_id=device(step),
-            device_id_type=MESH,
-        ).start()
-
-    others = gathered.at[pl.ds(0, (count - 1) * used)]
-    pltpu.make_async_copy(others, others, gather_recv).wait()
+        late[pl.ds(mine + c, 1), :] = line_of(c, 1)
+
+    send_all(late, 1)
 
     tiles = columns * count
     padded = round_up(tiles, LANES)
-    for h in range(QROWS):
-        parts = [
-            gathered[pl.ds(c * QROWS + h, count, stride=per_device), :] for c in range(columns)
-        ]
+
+    def receive(ref, h):
+        wait_all(ref, gather_recv.at[h])
+        parts = [ref[pl.ds(c, count, stride=per_device), :] for c in range(columns)]
         if padded > tiles:
             parts.append(jnp.zeros((padded - tiles, LANES), jnp.float32))
         table[h * LANES : (h + 1) * LANES, :] = jnp.concatenate(parts, axis=0).T
+
+    receive(early, 0)
 
     sublane = lax.broadcasted_iota(jnp.int32, (SUB, padded), 0)
     place = lax.broadcasted_iota(jnp.int32, (SUB, padded), 1)
@@ -402,23 +410,29 @@
         column + jnp.where(pick, stiffness, 0.0)
         for pick, column in zip(picks, block_at(SUM_AT, own_field))
     ]
-    load = stacked([PULL_A_AT + i for i in range(6)])
-    couplings = []
+    offsets = []
     for kind in range(KINDS):
         by = shifts[kind]
         du, dv = entry(OFFSET_AT + 2 * kind), entry(OFFSET_AT + 2 * kind + 1)
         offset = jnp.where(picks[0] | picks[3], du, jnp.where(picks[1] | picks[4], dv, 0.0))
+        offsets.append(offset)
         offset_b = to_next(offset, by)
         there_b = to_next(jnp.broadcast_to(entry(EXISTS_AT + kind), offset.shape), by)
         block_b = shift_columns(block_at(SELF_AT[kind], own_field), offset_b)
         for j in range(6):
             diagonal[j] = diagonal[j] + there_b * shift_rows(block_b[j], offset_b)
+
+    inverse = inverse_columns(diagonal, sublane)
+
+    receive(late, 1)
+    load = stacked([PULL_A_AT + i for i in range(6)])
+    couplings = []
+    for kind in range(KINDS):
+        by, offset = shifts[kind], offsets[kind]
         pull_b = stacked([PULL_B_AT + 6 * kind + i for i in range(6)])
         load = load + to_next(shift_rows(pull_b, offset), by)
         coupling = shift_columns(block_at(PAIR_AT[kind], pair_field), offset)
         couplings.append((coupling, transposed_columns(coupling, sublane), by))
-
-    inverse = inverse_columns(diagonal, sublane)
 
     def multiply(vector):
         result = apply_columns(diagonal, vector)
@@ -457,7 +471,8 @@
             line = jnp.sum(jnp.where(turn, own, 0.0), axis=0, keepdims=True)
             out_ref[index, c : c + 1, :] = line[:, 0:6]
 
-    pltpu.make_async_copy(others, others, gather_send).wait()
+    wait_all(early, gather_send.at[0])
+    wait_all(late, gather_send.at[1])
     for kind in range(2):
 
         @pl.when(sends[kind])
@@ -471,7 +486,7 @@
     sections = lax.axis_size("sec")
     tile_rows = lax.axis_size("tile")
     count = sections * tile_rows
-    per_device = round_up(columns * QROWS, SUB)
+    per_device = round_up(columns, SUB)
     held = columns * (IMAGES + 2) * height
     padded = round_up(columns * count, LANES)
     both = pl.pallas_call(
@@ -486,6 +501,7 @@
             pltpu.VMEM((held, width), jnp.float32),
             pltpu.VMEM((columns * QROWS * LANES, LANES), jnp.float32),
             pltpu.VMEM((count * per_device, LANES), jnp.float32),
+            pltpu.VMEM((count * per_device, LANES), jnp.float32),
             pltpu.VMEM((QROWS * LANES, padded), jnp.float32),
             pltpu.SMEM((columns, KINDS), jnp.int32),
             pltpu.SMEM((columns, 2, KINDS), jnp.int32),
@@ -493,11 +509,11 @@
             pltpu.SemaphoreType.DMA((4,)),
             pltpu.SemaphoreType.DMA((2, columns)),
             pltpu.SemaphoreType.DMA((2, columns)),
-            pltpu.SemaphoreType.DMA,
-            pltpu.SemaphoreType.DMA,
+            pltpu.SemaphoreType.DMA((2,)),
+            pltpu.SemaphoreType.DMA((2,)),
         ],
         compiler_params=pltpu.CompilerParams(
-            collective_id=0, has_side_effects=True, vmem_limit_bytes=60 * 1024 * 1024
+            collective_id=0, has_side_effects=True, vmem_limit_bytes=54784 * 1024
         ),
     )(
         tile_strips[0, 0],

time: 19.7 us -> 19.2 us (0.975)
  Pallas kernels: 17.7 us -> 17.1 us
    unnamed x0 -> x6, local copies, waits for them, and re-layouts: none -> 0.67 us
    squeeze x1, local copies, waits for them, and re-layouts: 1.24 us -> 0.57 us  [shards(): return (both[0], both[1])]
    pallas_call x1, Pallas kernels: 17.7 us -> 17.1 us  [shards(): pl.pallas_call(functools.partial(kernel, sections, tile_rows), out_shape=...]
where the time goes in v5:
time: 19.2 us; the launch traced here: 19.1 us
  Pallas kernels  17.1 us (89%)
  local copies, waits for them, and re-layouts  1.24 us (6%)
  between operations  0.66 us (3%)
    pallas_call x1, Pallas kernels, shards(): pl.pallas_call(functools.partial(kernel, sections, tile_rows), out_shape=...  17.1 us
    unnamed x6, local copies, waits for them, and re-layouts  0.67 us
    squeeze x1, local copies, waits for them, and re-layouts, shards(): return (both[0], both[1])  0.57 us

profile of v5, /device:TPU:0, one launch (start us, length us, event | category | flops | bytes accessed | tf_op | source)
XLA Modules:
  0.0 19.1 jit_solution(6713390631300316473)
XLA Ops:
  0.6 0.0 copy-start
  0.6 0.0 copy-start.1
  0.7 0.0 copy-start.2
  0.7 0.7 %copy-done = s32[1,1,2,3,2]{3,4,2,1,0:T(2,128)S(1)} copy-done((s32[1,1,2,3,2]{3,4,2,1,0:T(2,128)S(1)}, s32[1,1,2,3,2]{3,4,2,1,0:T(2,128)}, u32[]{:S(2)}) %copy-start) | copy-done | bytes 72
  1.3 0.0 copy-done.1
  1.3 0.0 copy-done.2
  1.3 17.1 %shard_map.59 = f32[2,2,6]{2,1,0:T(2,128)S(1)} custom-call(bf16[2,5,64,512]{3,2,1,0:T(8,128)(2,1)} %bitcast.15, s32[2,3]{1,0:T(2,128)S(1)} %bitcast.13, s32[2,2,3]{2,1,0:T(2,128)S(1)} %bitcast.12, f32[2]{0:T(128)S(1)} %bitcast.14), custom_call_target="tpu_custom_call" | custom-call | tf_op jit(solution)/shard_map/pallas_call | solution.py:492
  18.5 0.6 %slice_bitcast_fusion = (f32[6,1,1,2]{0,3,2,1:T(2,128)}, f32[6,1,1,2]{0,3,2,1:T(2,128)}) fusion(f32[2,6,2]{1,2,0:T(2,128)S(1)} %bitcast.11), kind=kLoop, calls=%fused_computation | loop fusion | bytes 192 | tf_op jit(solution)/shard_map/squeeze | solution.py:525
Async XLA Ops:
  0.6 0.7 %copy-start = (s32[1,1,2,3,2]{3,4,2,1,0:T(2,128)S(1)}, s32[1,1,2,3,2]{3,4,2,1,0:T(2,128)}, u32[]{:S(2)}) copy-start(s32[1,1,2,3,2]{3,4,2,1,0:T(2,128)} %param.6) | copy-start | bytes 148
  0.6 0.7 %copy-start.1 = (s32[1,1,2,3]{3,2,1,0:T(2,128)S(1)}, s32[1,1,2,3]{3,2,1,0:T(2,128)}, u32[]{:S(2)}) copy-start(s32[1,1,2,3]{3,2,1,0:T(2,128)} %param.5) | copy-start | bytes 76
  0.7 0.7 %copy-start.2 = (f32[1,1,2]{2,1,0:T(1,128)S(1)}, f32[1,1,2]{2,1,0:T(1,128)}, u32[]{:S(2)}) copy-start(f32[1,1,2]{2,1,0:T(1,128)} %param.7) | copy-start | bytes 28

commit v6 on v5

--- a/solution.py
+++ b/solution.py
@@ -141,6 +141,7 @@
     strip_recv,
     gather_send,
     gather_recv,
+    all_in,
 ):
     columns, _, height, width = strips.shape
     count = sections * tile_rows
@@ -155,11 +156,21 @@
         other = lax.rem(me + step, count)
         return (other // tile_rows, lax.rem(other, tile_rows))
 
+    def along_tile(step):
+        return (section, lax.rem(tile_row + step, tile_rows))
+
+    def along_sec(step):
+        return (lax.rem(section + step, sections), tile_row)
+
     barrier = pltpu.get_barrier_semaphore()
 
-    @pl.loop(1, count)
-    def _(step):
-        pl.semaphore_signal(barrier, inc=1, device_id=device(step), device_id_type=MESH)
+    def greet(semaphore, size, target):
+        @pl.loop(1, size)
+        def _(step):
+            pl.semaphore_signal(semaphore, inc=1, device_id=target(step), device_id_type=MESH)
+
+    greet(barrier, sections, along_sec)
+    greet(barrier, tile_rows, along_tile)
 
     local = [
         pltpu.make_async_copy(source, target, local_sem.at[index])
@@ -181,7 +192,7 @@
     down = jnp.where(gap == 1, 0.5, jnp.where(gap == -1, -0.5, 0.0)).astype(jnp.bfloat16)
     rows[...] = jnp.zeros_like(rows)
 
-    pl.semaphore_wait(barrier, count - 1)
+    pl.semaphore_wait(barrier, tile_rows + sections - 2)
 
     def strip_copy(kind, c):
         target = (section, tile_row - 1) if kind == 0 else (section - 1, tile_row)
@@ -202,6 +213,8 @@
         def _():
             for c in range(columns):
                 strip_copy(kind, c).start()
+
+    greet(all_in, tile_rows, along_tile)
 
     for copy in local:
         copy.wait()
@@ -329,6 +342,7 @@
         others = ref.at[pl.ds(0, (count - 1) * columns)]
         pltpu.make_async_copy(others, others, sem).wait()
 
+    pl.semaphore_wait(all_in, tile_rows - 1)
     send_all(early, 0)
 
     for kind in (1, 0):
@@ -511,6 +525,7 @@
             pltpu.SemaphoreType.DMA((2, columns)),
             pltpu.SemaphoreType.DMA((2,)),
             pltpu.SemaphoreType.DMA((2,)),
+            pltpu.SemaphoreType.REGULAR,
         ],
         compiler_params=pltpu.CompilerParams(
             collective_id=0, has_side_effects=True, vmem_limit_bytes=54784 * 1024

time: 19.2 us -> 18 us (0.938)
  Pallas kernels: 17.1 us -> 15.9 us
    pallas_call x1, Pallas kernels: 17.1 us -> 15.9 us  [shards(): pl.pallas_call(functools.partial(kernel, sections, tile_rows), out_shape=...]
where the time goes in v6:
time: 18 us; the launch traced here: 17.8 us
  Pallas kernels  15.9 us (88%)
  local copies, waits for them, and re-layouts  1.24 us (7%)
  between operations  0.66 us (4%)
    pallas_call x1, Pallas kernels, shards(): pl.pallas_call(functools.partial(kernel, sections, tile_rows), out_shape=...  15.9 us
    unnamed x6, local copies, waits for them, and re-layouts  0.67 us
    squeeze x1, local copies, waits for them, and re-layouts, shards(): return (both[0], both[1])  0.57 us

profile of v6, /device:TPU:0, one launch (start us, length us, event | category | flops | bytes accessed | tf_op | source)
XLA Modules:
  0.0 17.8 jit_solution(5712904284941166084)
XLA Ops:
  0.6 0.0 copy-start
  0.6 0.0 copy-start.1
  0.7 0.0 copy-start.2
  0.7 0.7 %copy-done = s32[1,1,2,3,2]{3,4,2,1,0:T(2,128)S(1)} copy-done((s32[1,1,2,3,2]{3,4,2,1,0:T(2,128)S(1)}, s32[1,1,2,3,2]{3,4,2,1,0:T(2,128)}, u32[]{:S(2)}) %copy-start) | copy-done | bytes 72
  1.3 0.0 copy-done.1
  1.3 0.0 copy-done.2
  1.3 15.9 %shard_map.59 = f32[2,2,6]{2,1,0:T(2,128)S(1)} custom-call(bf16[2,5,64,512]{3,2,1,0:T(8,128)(2,1)} %bitcast.15, s32[2,3]{1,0:T(2,128)S(1)} %bitcast.13, s32[2,2,3]{2,1,0:T(2,128)S(1)} %bitcast.12, f32[2]{0:T(128)S(1)} %bitcast.14), custom_call_target="tpu_custom_call" | custom-call | tf_op jit(solution)/shard_map/pallas_call | solution.py:506
  17.3 0.6 %slice_bitcast_fusion = (f32[6,1,1,2]{0,3,2,1:T(2,128)}, f32[6,1,1,2]{0,3,2,1:T(2,128)}) fusion(f32[2,6,2]{1,2,0:T(2,128)S(1)} %bitcast.11), kind=kLoop, calls=%fused_computation | loop fusion | bytes 192 | tf_op jit(solution)/shard_map/squeeze | solution.py:540
Async XLA Ops:
  0.6 0.7 %copy-start = (s32[1,1,2,3,2]{3,4,2,1,0:T(2,128)S(1)}, s32[1,1,2,3,2]{3,4,2,1,0:T(2,128)}, u32[]{:S(2)}) copy-start(s32[1,1,2,3,2]{3,4,2,1,0:T(2,128)} %param.6) | copy-start | bytes 148
  0.6 0.7 %copy-start.1 = (s32[1,1,2,3]{3,2,1,0:T(2,128)S(1)}, s32[1,1,2,3]{3,2,1,0:T(2,128)}, u32[]{:S(2)}) copy-start(s32[1,1,2,3]{3,2,1,0:T(2,128)} %param.5) | copy-start | bytes 76
  0.7 0.7 %copy-start.2 = (f32[1,1,2]{2,1,0:T(1,128)S(1)}, f32[1,1,2]{2,1,0:T(1,128)}, u32[]{:S(2)}) copy-start(f32[1,1,2]{2,1,0:T(1,128)} %param.7) | copy-start | bytes 28
